TPU v7x, 128 devices: a whole 4x4x4 slice. The times are simulated.
128 devices in a mesh: ctx: 2 (over z_hi), fsdp: 4 (over x), rep: 16 (over y, z_lo, core).
Axes of the slice: x: 4, y: 4, z: 4 (z_hi: 2, z_lo: 2; z = z_hi * 2 + z_lo), core: 2. Of those that a mesh axis runs over, the one named last changes fastest.
Arguments:
- tokens: bfloat16 [64, 512, 1536], P(('fsdp', 'rep'), 'ctx'), may hold values from -6 to 6
- segments: int32 [64, 512], P(('fsdp', 'rep')), may hold values from 0 to 3, as said below
- cotangent: bfloat16 [64, 512, 1536], P(('fsdp', 'rep'), 'ctx'), may hold values from -6 to 6
- gate_proj: bfloat16 [1536, 3072], P('fsdp'), may hold values from -0.15625 to 0.15625
- mixer_proj: bfloat16 [1536, 3328], P('fsdp'), may hold values from -0.15625 to 0.15625
- step_proj: bfloat16 [1536, 48], P('fsdp'), may hold values from -0.15625 to 0.15625
- final_proj: bfloat16 [3072, 1536], P('fsdp'), may hold values from -0.109375 to 0.109375
- norm_gain: float32 [1536], replicated, may hold values from 0.5 to 1.5
- conv_kernel: float32 [4, 3328], replicated, may hold values from -3 to 3
- conv_bias: float32 [3328], replicated, may hold values from -3 to 3
- step_offset: float32 [48], replicated, may hold values from -4.5 to -2
- log_rates: float32 [48], replicated, may hold values from -3 to 0.5
- skip_gain: float32 [48], replicated, may hold values from 0.5 to 1.5
- gating_gain: float32 [3072], replicated, may hold values from 0.5 to 1.5
Outputs:
- layer_out: float32 [64, 512, 1536], P(('fsdp', 'rep'), 'ctx')
- grad_tokens: float32 [64, 512, 1536], P(('fsdp', 'rep'), 'ctx')
- grad_gate: float32 [1536, 3072], P('fsdp')
- grad_mixer: float32 [1536, 3328], P('fsdp')
- grad_step: float32 [1536, 48], P('fsdp')
- grad_final: float32 [3072, 1536], P('fsdp')
- grad_norm: float32 [1536], replicated
- grad_kernel: float32 [4, 3328], replicated
- grad_bias: float32 [3328], replicated
- grad_offset: float32 [48], replicated
- grad_rates: float32 [48], replicated
- grad_skip: float32 [48], replicated
- grad_gating: float32 [3072], replicated
Inputs may be any that keep to these rules, and one draw needn't show every extreme that they name: `segments`: segment numbers of a sequence start at 0, never fall and rise by one at exactly three positions, so every sequence holds four documents; no document begins at positions k * 256 - 3 to k * 256 + 3.
All inputs are finite; a program needn't handle non-finite values.
Results may differ from a plain program's by a relative error of at most 0.02.
Values may be sent and summed in bfloat16 or wider, within the bound.
No kernel may reach another device: no remote copies, remote signals or barrier semaphores. Data moves between devices by JAX's collectives and lax.ppermute only.
A program may use at most 256 MiB of HBM per device.

v0:
```python
import jax
import jax.numpy as jnp
from jax import lax
from jax.sharding import PartitionSpec as P

INNER = 3072
STATE = 128
HEAD_DIM = 64
CONV_K = 4
HEADS = 48
CONV_CH = 3328


HIGH = lax.Precision.HIGHEST
eps = 1e-05


def passed_along(value, axis, steps):
    count = lax.axis_size(axis)
    leading, last = (max(0, -steps), min(count, count - steps))
    return lax.ppermute(value, axis, [(source, source + steps) for source in range(leading, last)])


def entering(value, axis, join, neutral, backward):
    count, mine = (lax.axis_size(axis), lax.axis_index(axis))
    pieces = jax.tree.map(lambda part: lax.all_gather(part, axis), value)
    if backward:
        pieces = jax.tree.map(lambda part: part[::-1], pieces)
        mine = count - 1 - mine
    so_far = jax.tree.map(
        lambda part, zero: jnp.full_like(part, 0) + jnp.asarray(zero, part.dtype), value, neutral
    )

    def step(position, so_far):
        longer = join(so_far, jax.tree.map(lambda part: part[position], pieces))
        return jax.tree.map(lambda new, old: jnp.where(position < mine, new, old), longer, so_far)

    return lax.fori_loop(0, count - 1, step, so_far)


def product(left, right):
    return jnp.dot(left, right, preferred_element_type=jnp.float32)


def times_transposed(left, right):
    return lax.dot_general(
        left, right, (((1,), (1,)), ((), ())), preferred_element_type=jnp.float32
    )


def transposed_times(left, right):
    return lax.dot_general(
        left, right, (((0,), (0,)), ((), ())), preferred_element_type=jnp.float32
    )


def tiny_norm(values, gain_vec):
    inverse_rms = lax.rsqrt(jnp.mean(values * values, -1, keepdims=True) + eps)
    return values * inverse_rms * gain_vec


def conv_local(row_block, prev_rows, conv_kernel, conv_bias, keepings):
    extended = jnp.concatenate([prev_rows, row_block], axis=1)
    length = row_block.shape[1]
    accumulated = conv_bias
    for lag in range(CONV_K):
        offset = CONV_K - 1 - lag
        accumulated = (
            accumulated
            + conv_kernel[lag] * extended[:, offset : offset + length] * keepings[lag][..., None]
        )
    return jax.nn.silu(accumulated)


def split_inputs(conv_out, step_raw, step_offset, log_rates):
    head_values = conv_out[:, :INNER].reshape(conv_out.shape[0], HEADS, HEAD_DIM)
    in_basis = conv_out[:, INNER : INNER + STATE]
    out_basis = conv_out[:, INNER + STATE :]
    step_size = jax.nn.softplus(step_raw + step_offset)
    decay_rate = step_size * -jnp.exp(log_rates)
    return (head_values, in_basis, out_basis, step_size, decay_rate)


def span_step(
    state_now, last_seg, head_values, in_basis, out_basis, step_size, decay_rate, segment, skip_gain
):
    size = segment.shape[0]
    cumulative = jnp.cumsum(decay_rate, axis=0)
    positions = jnp.arange(size)
    keeping = (segment[:, None] == segment[None, :]) & (positions[:, None] >= positions[None, :])
    gaps = jnp.where(keeping[..., None], cumulative[:, None, :] - cumulative[None, :, :], 0.0)
    mixing = jnp.where(keeping[..., None], jnp.exp(gaps), 0.0)
    scores = jnp.dot(out_basis, in_basis.T, precision=HIGH)
    weights = mixing * scores[..., None] * step_size[None, :, :]
    result = jnp.einsum("tsh,shp->thp", weights, head_values, precision=HIGH)
    entry_gate = (segment == last_seg).astype(jnp.float32)[:, None] * jnp.exp(cumulative)
    result = result + entry_gate[..., None] * jnp.einsum(
        "tn,hpn->thp", out_basis, state_now, precision=HIGH
    )
    result = result + skip_gain[None, :, None] * head_values
    tail_weight = (
        (segment == segment[-1]).astype(jnp.float32)[:, None]
        * jnp.exp(cumulative[-1][None, :] - cumulative)
        * step_size
    )
    fresh_state = jnp.einsum("sh,shp,sn->hpn", tail_weight, head_values, in_basis, precision=HIGH)
    carry_gate = (segment[-1] == last_seg).astype(jnp.float32) * jnp.exp(cumulative[-1])
    return (result, fresh_state + carry_gate[:, None, None] * state_now, segment[-1])


def local_scan(conv_out, step_raw, segment, prior_seg, step_offset, log_rates, skip_gain):
    head_values, in_basis, out_basis, step_size, decay_rate = split_inputs(
        conv_out, step_raw, step_offset, log_rates
    )
    state_now = jnp.zeros((HEADS, HEAD_DIM, STATE), jnp.float32)
    last_seg = jnp.array(-1, jnp.int32)
    result, state_now, last_seg = span_step(
        state_now,
        last_seg,
        head_values,
        in_basis,
        out_basis,
        step_size,
        decay_rate,
        segment,
        skip_gain,
    )
    outputs = [result]
    through = jnp.exp(jnp.sum(decay_rate, axis=0)) * (segment[-1] == prior_seg).astype(jnp.float32)
    return (jnp.concatenate(outputs, axis=0), state_now, through)


def carried_in(conv_out, step_raw, segment, prior_seg, step_offset, log_rates, state_in):
    _, _, out_basis, _, decay_rate = split_inputs(conv_out, step_raw, step_offset, log_rates)
    cumulative = jnp.cumsum(decay_rate, axis=0)
    entry_gate = (segment == prior_seg).astype(jnp.float32)[:, None] * jnp.exp(cumulative)
    return entry_gate[..., None] * jnp.einsum("tn,hpn->thp", out_basis, state_in, precision=HIGH)


def combine_states(earlier, later):
    return (earlier[0] * later[0], later[0][..., None, None] * earlier[1] + later[1])


def per_device(
    tokens,
    segments,
    cotangent,
    gate_proj,
    mixer_proj,
    step_proj,
    final_proj,
    norm_gain,
    conv_kernel,
    conv_bias,
    step_offset,
    log_rates,
    skip_gain,
    gating_gain,
):
    sequences, length, model_width = tokens.shape
    row_count = sequences * length
    full_gate, full_mixer, full_step, full_final = (
        lax.all_gather(gate_proj, "fsdp", axis=0, tiled=True),
        lax.all_gather(mixer_proj, "fsdp", axis=0, tiled=True),
        lax.all_gather(step_proj, "fsdp", axis=0, tiled=True),
        lax.all_gather(final_proj, "fsdp", axis=0, tiled=True),
    )
    tokens_f = tokens.astype(jnp.float32).reshape(row_count, model_width)
    normed_f, pull_norm = jax.vjp(tiny_norm, tokens_f, norm_gain)
    normed = normed_f.astype(jnp.bfloat16)
    gate_val = product(normed, full_gate)
    mixer_in = product(normed, full_mixer).astype(jnp.bfloat16)
    step_raw = product(normed, full_step)
    mixer_rows = mixer_in.reshape(sequences, length, CONV_CH)
    prev_rows = passed_along(mixer_rows[:, length - CONV_K + 1 :], "ctx", 1)
    lead_seg = jnp.full((sequences, CONV_K - 1), -1, jnp.int32)
    padded = jnp.concatenate([lead_seg, segments], axis=1)
    window = lax.dynamic_slice_in_dim(
        padded, lax.axis_index("ctx") * length, length + CONV_K - 1, axis=1
    )
    own_seg = window[:, CONV_K - 1 :]
    prior_seg = window[:, CONV_K - 2]
    keepings = [
        (window[:, CONV_K - 1 - lag : CONV_K - 1 - lag + length] == own_seg).astype(jnp.float32)
        for lag in range(CONV_K)
    ]

    def conv_part(row_block, halo_rows, kernel_taps, bias_vec):
        return conv_local(row_block, halo_rows, kernel_taps, bias_vec, keepings)

    conv_out, pull_conv = jax.vjp(
        conv_part,
        mixer_rows.astype(jnp.float32),
        prev_rows.astype(jnp.float32),
        conv_kernel,
        conv_bias,
    )
    step_rows = step_raw.reshape(sequences, length, HEADS)

    def first_part(conv_vals, step_vals, offset_vec, rate_vec, skip_vec):
        return jax.vmap(local_scan, in_axes=(0, 0, 0, 0, None, None, None))(
            conv_vals, step_vals, own_seg, prior_seg, offset_vec, rate_vec, skip_vec
        )

    (y_local, state_local, through), pull_first = jax.vjp(
        first_part, conv_out, step_rows, step_offset, log_rates, skip_gain
    )
    unit_gates = jnp.ones_like(through)
    zero_state = jnp.zeros_like(state_local)
    _, state_in = entering(
        (through, state_local), "ctx", combine_states, (unit_gates, zero_state), False
    )

    def second_part(conv_vals, step_vals, offset_vec, rate_vec, incoming):
        return jax.vmap(carried_in, in_axes=(0, 0, 0, 0, None, None, 0))(
            conv_vals, step_vals, own_seg, prior_seg, offset_vec, rate_vec, incoming
        )

    y_in, pull_second = jax.vjp(second_part, conv_out, step_rows, step_offset, log_rates, state_in)
    y_all = (y_local + y_in).reshape(row_count, INNER)

    def gate_part(y_vals, gate_vals, gain_vec):
        return tiny_norm(y_vals * jax.nn.silu(gate_vals), gain_vec)

    gated, pull_gate = jax.vjp(gate_part, y_all, gate_val, gating_gain)
    gated_low = gated.astype(jnp.bfloat16)
    layer_out = tokens_f + product(gated_low, full_final)
    cot_rows = cotangent.reshape(row_count, model_width)
    grad_final = transposed_times(gated_low, cot_rows)
    back_gate, back_mixer, back_step, back_final = (
        lax.all_gather(gate_proj, "fsdp", axis=0, tiled=True),
        lax.all_gather(mixer_proj, "fsdp", axis=0, tiled=True),
        lax.all_gather(step_proj, "fsdp", axis=0, tiled=True),
        lax.all_gather(final_proj, "fsdp", axis=0, tiled=True),
    )
    d_gated = times_transposed(cot_rows, back_final)
    d_y, d_gate, d_gating = pull_gate(d_gated)
    d_gate_low = d_gate.astype(jnp.bfloat16)
    d_heads = d_y.reshape(sequences, length, HEADS, HEAD_DIM)
    d_conv_b, d_step_b, d_offset_b, d_rates_b, d_state_in = pull_second(d_heads)
    _, d_later = entering(
        (through, d_state_in), "ctx", combine_states, (unit_gates, zero_state), True
    )
    d_through = jnp.sum(d_later * state_in, axis=(-2, -1))
    d_conv_a, d_step_a, d_offset_a, d_rates_a, d_skip = pull_first((d_heads, d_later, d_through))
    d_step_low = (d_step_a + d_step_b).reshape(row_count, HEADS).astype(jnp.bfloat16)
    d_mixer_rows, d_prev, d_kernel, d_bias = pull_conv(d_conv_a + d_conv_b)
    returned = passed_along(d_prev.astype(jnp.bfloat16), "ctx", -1).astype(d_prev.dtype)
    d_mixer_rows = jnp.concatenate(
        [d_mixer_rows[:, : length - CONV_K + 1], d_mixer_rows[:, length - CONV_K + 1 :] + returned],
        axis=1,
    )
    d_mixer_low = d_mixer_rows.reshape(row_count, CONV_CH).astype(jnp.bfloat16)
    d_normed = (
        times_transposed(d_gate_low, back_gate)
        + times_transposed(d_mixer_low, back_mixer)
        + times_transposed(d_step_low, back_step)
    )
    grad_gate = transposed_times(normed, d_gate_low)
    grad_mixer = transposed_times(normed, d_mixer_low)
    grad_step = transposed_times(normed, d_step_low)
    d_tokens, d_norm = pull_norm(d_normed)
    grad_tokens = cot_rows.astype(jnp.float32) + d_tokens
    owned = (
        lax.psum_scatter(
            grad_gate.astype(jnp.bfloat16), "fsdp", scatter_dimension=0, tiled=True
        ).astype(jnp.float32),
        lax.psum_scatter(
            grad_mixer.astype(jnp.bfloat16), "fsdp", scatter_dimension=0, tiled=True
        ).astype(jnp.float32),
        lax.psum_scatter(
            grad_step.astype(jnp.bfloat16), "fsdp", scatter_dimension=0, tiled=True
        ).astype(jnp.float32),
        lax.psum_scatter(
            grad_final.astype(jnp.bfloat16), "fsdp", scatter_dimension=0, tiled=True
        ).astype(jnp.float32),
    )
    summed = (
        lax.psum(owned[0].astype(jnp.bfloat16), ("ctx", "rep")).astype(jnp.float32),
        lax.psum(owned[1].astype(jnp.bfloat16), ("ctx", "rep")).astype(jnp.float32),
        lax.psum(owned[2].astype(jnp.bfloat16), ("ctx", "rep")).astype(jnp.float32),
        lax.psum(owned[3].astype(jnp.bfloat16), ("ctx", "rep")).astype(jnp.float32),
    )
    small = lax.psum(
        (
            d_norm,
            d_kernel,
            d_bias,
            d_offset_a + d_offset_b,
            d_rates_a + d_rates_b,
            d_skip,
            d_gating,
        ),
        ("ctx", "fsdp", "rep"),
    )
    return (
        layer_out.reshape(sequences, length, model_width),
        grad_tokens.reshape(sequences, length, model_width),
        summed[0],
        summed[1],
        summed[2],
        summed[3],
        small[0],
        small[1],
        small[2],
        small[3],
        small[4],
        small[5],
        small[6],
    )


def solution(mesh):
    return jax.shard_map(
        per_device,
        mesh=mesh,
        in_specs=(
            P(("fsdp", "rep"), "ctx", None),
            P(("fsdp", "rep"), None),
            P(("fsdp", "rep"), "ctx", None),
            P("fsdp", None),
            P("fsdp", None),
            P("fsdp", None),
            P("fsdp", None),
            P(),
            P(),
            P(),
            P(),
            P(),
            P(),
            P(),
        ),
        out_specs=(
            P(("fsdp", "rep"), "ctx", None),
            P(("fsdp", "rep"), "ctx", None),
            P("fsdp", None),
            P("fsdp", None),
            P("fsdp", None),
            P("fsdp", None),
            P(),
            P(),
            P(),
            P(),
            P(),
            P(),
            P(),
        ),
        check_vma=False,
    )
```

profile of v0, /device:TPU:0, one launch (start us, length us, event | category | flops | bytes accessed | tf_op | source)
XLA Modules:
  0.0 1056.0 jit_solution(3793147746323265691)
XLA Ops:
  8.0 12.7 %all_gather.35 = bf16[1536,48]{0,1:T(8,128)(2,1)S(1)} all-gather(bf16[384,48]{0,1:T(8,128)(2,1)} %param.20), channel_id=1, replica_groups=mesh['ctx'=2,'fsdp'=4,'rep'=16] {'fsdp'}, dimensions={0}, use_global_device_ids=true | all-gather | bytes 184320 | tf_op jit(solution)/shard_map/all_gather | solution.py:165
  28.2 82.6 %all-gather.9.cloned.1.call-done = bf16[1536,3328]{1,0:T(8,128)(2,1)} async-done(((bf16[384,3328]{1,0:T(8,128)(2,1)}), bf16[1536,3328]{1,0:T(8,128)(2,1)}) %all-gather.9.cloned.1.call-update) | async-done | bytes 10223632 | tf_op jit(solution)/shard_map/all_gather | solution.py:164
  110.9 6.8 convolution_convert_fusion.3
  154.8 7.0 all-reduce.15
  170.4 20.1 %all-gather.15.cloned.1.call-done = f32[96,64,128]{2,1,0:T(8,128)} async-done(((f32[48,64,128]{2,1,0:T(8,128)}), f32[96,64,128]{2,1,0:T(8,128)}) %all-gather.15.cloned.1.call-update) | async-done | bytes 3145744 | tf_op jit(solution)/shard_map/all_gather | solution.py:26
  195.0 16.2 %fusion.32 = f32[1,256,48,64]{1,3,2,0:T(8,128)} fusion(f32[256,48,64]{0,2,1:T(8,128)S(1)} %fusion.75, f32[1,256,48,64]{1,3,2,0:T(8,128)S(1)} %bitcast.429, f32[256,48,64]{0,2,1:T(8,128)S(1)} %copy-done.15, f32[256,48,64]{0,2,1:T(8,128)S(1)} %bitcast.428, f32[256,48]{0,1:T(8,128)S(1)} %copy-done.55, f32[256,256]{1,0:T(8,128)S(1)} %copy-done.30, ...), kind=kOutput, calls=%fused_computation.62 | convolution fusion | flops 2436366336 | bytes 16253120 | tf_op jit(solution)/shard_map/jvp(vmap(tsh,shp->thp))/dot_general | solution.py:95
  214.8 68.6 %all-gather.11.cloned.1.call-done = bf16[1536,3072]{1,0:T(8,128)(2,1)} async-done(((bf16[384,3072]{1,0:T(8,128)(2,1)}), bf16[1536,3072]{1,0:T(8,128)(2,1)}) %all-gather.11.cloned.1.call-update) | async-done | bytes 9437200 | tf_op jit(solution)/shard_map/all_gather | solution.py:163
  283.4 10.5 multiply_reduce_fusion.9
  293.9 84.0 %all-gather.13.cloned.1.call-done = bf16[3072,1536]{1,0:T(8,128)(2,1)} async-done(((bf16[768,1536]{1,0:T(8,128)(2,1)}), bf16[3072,1536]{1,0:T(8,128)(2,1)}) %all-gather.13.cloned.1.call-update) | async-done | bytes 9437200 | tf_op jit(solution)/shard_map/all_gather | solution.py:166
  377.9 9.9 multiply_reduce_fusion.5
  397.4 13.1 %copy.161 = f32[256,3072]{0,1:T(8,128)} copy(f32[256,3072]{1,0:T(8,128)} %mul.852) | data formatting | bytes 6291456 | tf_op jit(solution)/shard_map/transpose(jvp(vmap()))/mul | solution.py:137
  416.3 8.5 convolution_convert_fusion.1
  424.8 8.2 convolution_convert_fusion.2
  436.7 22.6 %fusion.5 = (f32[256,48]{0,1:T(8,128)}, f32[256,48]{0,1:T(8,128)}, f32[256,48]{0,1:T(8,128)}, f32[256,256]{1,0:T(8,128)S(1)}) fusion(f32[256,256]{1,0:T(8,128)} %fusion.150, f32[256,48]{0,1:T(8,128)} %copy.148, f32[256,48]{0,1:T(8,128)} %copy.146, pred[256,256]{1,0:T(8,128)(4,1)S(1)} %copy-done.51, f32[48,64,256]{2,1,0:T(8,128)} %bitcast.433, ...), kind=kOutput, calls=%fused_computation.14 | convolution fusion | flops 2463002624 | bytes 7127040 | tf_op jit(solution)/shard_map/transpose(jvp(vmap(tsh,shp->thp)))/dot_general | solution.py:95
  467.9 5.9 fusion.94
  479.0 12.4 %bitcast_add_fusion = f32[1,256,48,64]{1,3,2,0:T(8,128)} fusion(f32[48,64,256]{2,1,0:T(8,128)S(1)} %get-tuple-element.130, f32[256,48,64]{0,2,1:T(8,128)S(1)} %bitcast.435, f32[48,64,256]{2,1,0:T(8,128)S(1)} %bitcast.436, f32[256,48]{0,1:T(8,128)S(1)} %copy-done.56, f32[256,256]{1,0:T(8,128)S(1)} %copy-done.31, f32[256,48]{0,1:T(8,128)S(1)} %copy-done.58, ...), kind=kOutput, calls=%fused_computation.59 | convolution fusion | flops 2434793472 | bytes 13058240 | tf_op jit(solution)/shard_map/transpose(jvp(vmap(tsh,shp->thp)))/dot_general | solution.py:95
  495.1 6.7 fusion.102
  501.9 7.0 multiply_reduce_fusion.4
  547.5 9.5 reduce-scatter.11.cloned.1.call-done
  557.0 91.2 %reduce-scatter.7.cloned.1.call-done = bf16[384,3072]{1,0:T(8,128)(2,1)} async-done(((bf16[1536,3072]{1,0:T(8,128)(2,1)}), bf16[384,3072]{1,0:T(8,128)(2,1)}) %reduce-scatter.7.cloned.1.call-update) | async-done | bytes 2359312 | tf_op jit(solution)/shard_map/reduce_scatter | solution.py:265
  648.2 97.6 %reduce-scatter.9.cloned.1.call-done = bf16[384,3328]{1,0:T(8,128)(2,1)} async-done(((bf16[1536,3328]{1,0:T(8,128)(2,1)}), bf16[384,3328]{1,0:T(8,128)(2,1)}) %reduce-scatter.9.cloned.1.call-update) | async-done | bytes 2555920 | tf_op jit(solution)/shard_map/reduce_scatter | solution.py:268
  746.5 8.6 fusion.44
  771.8 129.4 %psum.79 = bf16[384,48]{0,1:T(8,128)(2,1)S(1)} all-reduce(bf16[384,48]{0,1:T(8,128)(2,1)S(1)} %copy.182), channel_id=1, replica_groups=mesh['ctx'=2,'fsdp'=4,'rep'=16] {'ctx','rep'}, use_global_device_ids=true, to_apply=%region_25.27 | all-reduce | flops 18432 | bytes 73728 | tf_op jit(solution)/shard_map/psum | solution.py:281
  911.9 128.4 %all-reduce.21.cloned.1.call-done = (f32[1536]{0:T(1024)}, f32[4,3328]{1,0:T(4,128)}, f32[3328]{0:T(1024)}, f32[48]{0:T(128)}, f32[48]{0:T(128)}, /*index=5*/f32[48]{0:T(128)}, f32[3072]{0:T(1024)}) async-done(((f32[1536]{0:T(1024)}, f32[4,3328]{1,0:T(4,128)}, f32[3328]{0:T(1024)}, f32[48]{0:T(128)}, f32[48]{0:T(128)}, /*index=5*/f32[48]{0:T(128)}, f32[3072]{0:T(1024)}), (f32[1536]{0:T(1024)}, ...) | async-done | bytes 85584 | tf_op jit(solution)/shard_map/psum | solution.py:284
  (331 shorter events, 170.3 us)
Async XLA Ops:
  7.2 103.6 %all-gather.9.cloned.1.call-start = ((), (), s32[]{:S(2)}) async-start(), calls=%async_computation.4 | async-start | bytes 12779520 | tf_op jit(solution)/shard_map/all_gather | solution.py:164
  8.0 182.5 %all-gather.15.cloned.1.call-start = ((), (), s32[]{:S(2)}) async-start(), calls=%async_computation.10 | async-start | bytes 4718592 | tf_op jit(solution)/shard_map/all_gather | solution.py:26
  20.8 96.9 %copy-start.24 = (bf16[1536,48]{0,1:T(8,128)(2,1)}, bf16[1536,48]{0,1:T(8,128)(2,1)S(1)}, u32[]{:S(2)}) copy-start(bf16[1536,48]{0,1:T(8,128)(2,1)S(1)} %all_gather.35) | copy-start | bytes 442372
  23.9 93.8 %copy-start.77 = (f32[48]{0:T(128)}, f32[48]{0:T(128)S(1)}, u32[]{:S(2)}) copy-start(f32[48]{0:T(128)S(1)} %slice_bitcast_fusion.3) | copy-start | bytes 580
  25.3 99.1 %copy-start.61 = (f32[1,256]{1,0:T(1,128)}, f32[1,256]{1,0:T(1,128)S(1)}, u32[]{:S(2)}) copy-start(f32[1,256]{1,0:T(1,128)S(1)} %get-tuple-element.121) | copy-start | bytes 3076
  25.3 99.1 %copy-start.63 = (f32[1,256]{1,0:T(1,128)}, f32[1,256]{1,0:T(1,128)S(1)}, u32[]{:S(2)}) copy-start(f32[1,256]{1,0:T(1,128)S(1)} %get-tuple-element.122) | copy-start | bytes 3076
  25.3 99.1 %copy-start.65 = (f32[1,256]{1,0:T(1,128)}, f32[1,256]{1,0:T(1,128)S(1)}, u32[]{:S(2)}) copy-start(f32[1,256]{1,0:T(1,128)S(1)} %get-tuple-element.123) | copy-start | bytes 3076
  27.7 96.7 %copy-start.36 = (f32[3328]{0:T(1024)}, f32[3328]{0:T(1024)S(1)}, u32[]{:S(2)}) copy-start(f32[3328]{0:T(1024)S(1)} %get-tuple-element.73) | copy-start | bytes 39940
  27.7 96.7 %copy-start.38 = (f32[3328]{0:T(1024)}, f32[3328]{0:T(1024)S(1)}, u32[]{:S(2)}) copy-start(f32[3328]{0:T(1024)S(1)} %get-tuple-element.74) | copy-start | bytes 39940
  27.7 96.7 %copy-start.40 = (f32[3328]{0:T(1024)}, f32[3328]{0:T(1024)S(1)}, u32[]{:S(2)}) copy-start(f32[3328]{0:T(1024)S(1)} %get-tuple-element.75) | copy-start | bytes 39940
  27.7 96.7 %copy-start.42 = (f32[3328]{0:T(1024)}, f32[3328]{0:T(1024)S(1)}, u32[]{:S(2)}) copy-start(f32[3328]{0:T(1024)S(1)} %get-tuple-element.76) | copy-start | bytes 39940
  117.8 6.6 collective-permute-start
  139.5 143.9 %all-gather.11.cloned.1.call-start = ((), (), s32[]{:S(2)}) async-start(), calls=%async_computation.5 | async-start | bytes 11796480 | tf_op jit(solution)/shard_map/all_gather | solution.py:163
  140.2 237.6 %all-gather.13.cloned.1.call-start = ((), (), s32[]{:S(2)}) async-start(), calls=%async_computation.6 | async-start | bytes 11796480 | tf_op jit(solution)/shard_map/all_gather | solution.py:166
  140.8 333.0 %all-gather.17.cloned.1.call-start = ((), (), s32[]{:S(2)}) async-start(), calls=%async_computation.11 | async-start | bytes 4718592 | tf_op jit(solution)/shard_map/all_gather | solution.py:26
  214.8 163.1 %copy-start.44 = (f32[3072]{0:T(1024)S(1)}, f32[3072]{0:T(1024)}, u32[]{:S(2)}) copy-start(f32[3072]{0:T(1024)} %param.28) | copy-start | bytes 36868
  293.9 122.4 %copy-start.69 = (f32[256]{0:T(256)}, f32[256]{0:T(256)S(1)}, u32[]{:S(2)}) copy-start(f32[256]{0:T(256)S(1)} %fusion.167) | copy-start | bytes 3076
  416.2 140.8 %reduce-scatter.11.cloned.1.call-start = ((), (), s32[]{:S(2)}) async-start(), calls=%async_computation.9 | async-start | bytes 11796480 | tf_op jit(solution)/shard_map/reduce_scatter | solution.py:274
  424.8 223.4 %reduce-scatter.7.cloned.1.call-start = ((), (), s32[]{:S(2)}) async-start(), calls=%async_computation.7 | async-start | bytes 11796480 | tf_op jit(solution)/shard_map/reduce_scatter | solution.py:265
  433.0 312.7 %reduce-scatter.9.cloned.1.call-start = ((), (), s32[]{:S(2)}) async-start(), calls=%async_computation.8 | async-start | bytes 12779520 | tf_op jit(solution)/shard_map/reduce_scatter | solution.py:268
  511.2 7.5 collective-permute-start.1
  524.4 246.4 %reduce-scatter.13.cloned.1.call-start = ((), (), s32[]{:S(2)}) async-start(), calls=%async_computation.12 | async-start | bytes 491520
  546.7 355.1 %all-reduce.23.cloned.1.call-start = ((), (), s32[]{:S(2)}) async-start(), calls=%async_computation.14 | async-start | bytes 14548992 | tf_op jit(solution)/shard_map/psum | solution.py:279
  745.8 294.5 %all-reduce.21.cloned.1.call-start = ((), (), s32[]{:S(2)}) async-start(), calls=%async_computation.13 | async-start | bytes 183296 | tf_op jit(solution)/shard_map/psum | solution.py:284
  (83 other events, 945.8 us)
Sparse Core Ops, SparseCore 0:
  9.7 101.0 all-gather.8
  139.6 50.8 all-gather.14
  192.2 91.1 all-gather.10
  284.9 92.9 all-gather.12
  416.3 50.0 all-gather.16
  468.8 88.1 reduce-scatter.10
  559.4 88.6 reduce-scatter.6
  650.6 95.0 reduce-scatter.8
  748.7 20.5 reduce-scatter.12
  773.5 118.9 all-reduce.22
  900.7 139.5 all-reduce.20
where the time goes:
time: 1070 us; the launch traced here: 1060 us
  waiting for transfers between devices  591 us (55%)
  matrix products  169 us (16%)
  blocking collectives  149 us (14%)
  local copies, waits for them, and re-layouts  65.7 us (6%)
  other arithmetic  56 us (5%)
  between operations  18.2 us (2%)
    psum x1, blocking collectives, per_device(): lax.psum(owned[2].astype(jnp.bfloat16), ('ctx', 'rep')).astype(jnp.float32)  129 us
    psum x1, waiting for transfers between devices, per_device(): lax.psum((d_norm, d_kernel, d_bias, d_offset_a + d_offset_b, d_rates_a +...  128 us
    reduce_scatter x1, waiting for transfers between devices, per_device(): lax.psum_scatter(grad_mixer.astype(jnp.bfloat16), 'fsdp', scatter_dimensi...  97.6 us
    reduce_scatter x1, waiting for transfers between devices, per_device(): lax.psum_scatter(grad_gate.astype(jnp.bfloat16), 'fsdp', scatter_dimensio...  91.2 us
    all_gather x1, waiting for transfers between devices, per_device(): lax.all_gather(final_proj, 'fsdp', axis=0, tiled=True)  84 us
    all_gather x1, waiting for transfers between devices, per_device(): lax.all_gather(mixer_proj, 'fsdp', axis=0, tiled=True)  82.6 us
    all_gather x1, waiting for transfers between devices, per_device(): lax.all_gather(gate_proj, 'fsdp', axis=0, tiled=True)  68.6 us
    dot_general x3, matrix products, span_step(): result = jnp.einsum('tsh,shp->thp', weights, head_values, precision=HIGH)  51.2 us
  transfers between devices with their start and end apart: 13, of which 10 were waited for; matrix products, arithmetic and copies ran while one was open for 21% of the time, Pallas kernels for 0%

commit v1 on v0

v1 whole, which is shorter than its diff:
```python
import functools

import jax
import jax.numpy as jnp
from jax import lax
from jax.experimental import pallas as pl
from jax.experimental.pallas import tpu as pltpu
from jax.sharding import PartitionSpec as P

D = 1536
INNER = 3072
STATE = 128
HEADS = 48
HEAD_DIM = 64
CONV_CH = 3328
LOCAL = 256
GROUP = 8
OWN = 6
HP = OWN * HEAD_DIM
CH = HP + 2 * STATE
ROWS = D // 4
EPS = 1e-05
F32 = jnp.float32
BF16 = jnp.bfloat16
HIGH = lax.Precision.HIGHEST
MASKED = -1e30
VMEM_LIMIT = 56 * 1024 * 1024


def x_shift(value, steps):
    return lax.ppermute(value, "fsdp", [(i, (i + steps) % 4) for i in range(4)])


def y_shift(value, steps):
    pairs = [(r, ((r // 4 + steps) % 4) * 4 + r % 4) for r in range(16)]
    return lax.ppermute(value, "rep", pairs)


def core_swap(value):
    return lax.ppermute(value, "rep", [(r, r ^ 1) for r in range(16)])


def z_swap(value, bit):
    if bit == 0:
        return lax.ppermute(value, "rep", [(r, r ^ 2) for r in range(16)])
    return lax.ppermute(value, "ctx", [(0, 1), (1, 0)])


def ring_gather(own, shift):
    half = own.shape[0] // 2
    below = shift(own, 1)
    above = shift(own, -1)
    far_a = shift(below[:half], 1)
    far_b = shift(above[half:], -1)
    return own, below, jnp.concatenate([far_a, far_b], axis=0), above


def ring_scatter(own, ahead, far, behind, shift):
    half = own.shape[0] // 2
    up = shift(far[:half], 1)
    down = shift(far[half:], -1)
    ahead = jnp.concatenate([ahead[:half] + up, ahead[half:]], axis=0)
    behind = jnp.concatenate([behind[:half], behind[half:] + down], axis=0)
    from_below = shift(ahead, 1)
    from_above = shift(behind, -1)
    return own.astype(F32) + from_below.astype(F32) + from_above.astype(F32)


def sum_z(value):
    value = value + z_swap(value, 0)
    return value + z_swap(value, 1)


def rolled(blocks, start, count):
    twice = jnp.concatenate([blocks, blocks], axis=0)
    return lax.dynamic_slice_in_dim(twice, start % 4, count, axis=0)


def mm(a, b, dims, precision=None):
    return lax.dot_general(a, b, (dims, ((), ())), precision=precision, preferred_element_type=F32)


NN = ((1,), (0,))
NT = ((1,), (1,))
TN = ((0,), (0,))


def lane_ids(rows, cols):
    return lax.broadcasted_iota(jnp.int32, (rows, cols), 1)


def pair(values, p, left):
    return jnp.where(left, values[:, 2 * p : 2 * p + 1], values[:, 2 * p + 1 : 2 * p + 2])


def triangle():
    row = lax.broadcasted_iota(jnp.int32, (LOCAL, LOCAL), 0)
    col = lax.broadcasted_iota(jnp.int32, (LOCAL, LOCAL), 1)
    return row >= col


def mask_bias(cols, rows):
    same = cols[:, 5:6] == rows[0:1, :]
    return jnp.where(same & triangle(), 0.0, MASKED)


def taps(x, halo, cols, k):
    ext = jnp.concatenate([halo, x], axis=0)
    return ext[8 - k : 8 - k + LOCAL] * cols[:, k - 1 : k]


def conv_kernel_fn(
    ctx_ref, xbc_ref, halo_ref, raw_ref, cols_ref, par_ref, hp_ref,
    u_ref, xc_ref, dt_ref, cum_ref, state_ref,
):
    x = xbc_ref[0].astype(F32)
    halo = halo_ref[0]
    cols = cols_ref[0]
    par = par_ref[...]
    hp = hp_ref[...]
    u = par[4:5] + par[0:1] * x
    for k in range(1, 4):
        u = u + par[k : k + 1] * taps(x, halo, cols, k)
    u_ref[0] = u
    xc = u * jax.nn.sigmoid(u)
    xc_ref[0] = xc.astype(BF16)
    raw = raw_ref[0] + hp[0:1]
    dt = jnp.maximum(raw, 0.0) + jnp.log1p(jnp.exp(-jnp.abs(raw)))
    dt_ref[0] = dt
    cum = mm(triangle().astype(F32), dt * hp[1:2], NN, HIGH)
    cum_ref[0] = cum

    @pl.when(ctx_ref[0] == 0)
    def _():
        weight = cols[:, 4:5] * jnp.exp(cum[LOCAL - 1 : LOCAL] - cum) * dt
        left = lane_ids(LOCAL, 128) < HEAD_DIM
        basis = xc[:, HP : HP + STATE].astype(BF16)
        for p in range(3):
            part = xc[:, 128 * p : 128 * p + 128] * pair(weight, p, left)
            state_ref[0, 128 * p : 128 * p + 128] = mm(part.astype(BF16), basis, TN).astype(BF16)

    @pl.when(ctx_ref[0] != 0)
    def _():
        state_ref[0] = jnp.zeros((HP, STATE), BF16)


def scan_kernel_fn(xc_ref, dt_ref, cum_ref, cols_ref, rows_ref, hp_ref, y_ref):
    xc = xc_ref[0]
    dt = dt_ref[0]
    cum = cum_ref[0]
    hp = hp_ref[...]
    cum_t = cum.T
    basis, out_basis = xc[:, HP : HP + STATE], xc[:, HP + STATE :]
    scores = mm(out_basis, basis, NT)
    bias = mask_bias(cols_ref[0], rows_ref[0])
    left = lane_ids(LOCAL, 128) < HEAD_DIM
    left1 = lane_ids(1, 128) < HEAD_DIM
    for p in range(3):
        x = xc[:, 128 * p : 128 * p + 128].astype(F32)
        scaled = (x * pair(dt, p, left)).astype(BF16)
        halves = []
        for h in (2 * p, 2 * p + 1):
            mix = jnp.exp(cum[:, h : h + 1] - cum_t[h : h + 1] + bias) * scores
            halves.append(mm(mix.astype(BF16), scaled, NN))
        y = jnp.where(left, halves[0], halves[1]) + pair(hp[2:3], p, left1) * x
        y_ref[0, :, 128 * p : 128 * p + 128] = y


def gate_kernel_fn(
    ctx_ref, y_ref, state_ref, z_ref, dmix_ref, xc_ref, cum_ref, cols_ref, gain_ref,
    yall_ref, sums_ref,
):
    yall_ref[0] = y_ref[0]

    @pl.when(ctx_ref[0] != 0)
    def _():
        out_basis = xc_ref[0][:, HP + STATE :]
        enter = cols_ref[0][:, 3:4] * jnp.exp(cum_ref[0])
        left = lane_ids(LOCAL, 128) < HEAD_DIM
        for p in range(3):
            at = slice(128 * p, 128 * p + 128)
            yall_ref[0, :, at] += pair(enter, p, left) * mm(out_basis, state_ref[0, at], NT)

    z = z_ref[0]
    gated = yall_ref[0] * (z * jax.nn.sigmoid(z))
    first = jnp.sum(gated * gated, axis=1, keepdims=True)
    second = jnp.sum(dmix_ref[0] * gain_ref[0:1] * gated, axis=1, keepdims=True)
    lane = lane_ids(LOCAL, 128)
    both = jnp.where(lane == 0, first, jnp.where(lane == 1, second, 0.0))
    sums_ref[0] = both.T[0:8]


def ungate_kernel_fn(
    ctx_ref, y_ref, z_ref, dmix_ref, sums_ref, xc_ref, cum_ref, cols_ref, gain_ref,
    mixed_ref, dy_ref, dz_ref, dstate_ref, dgain_ref,
):
    step = pl.program_id(0)
    pad = jnp.concatenate([sums_ref[0], jnp.zeros((120, LOCAL), F32)], axis=0).T
    inv = lax.rsqrt(pad[:, 0:1] / INNER + EPS)
    mean_ev = inv * pad[:, 1:2] / INNER
    y = y_ref[0]
    z = z_ref[0]
    dmix = dmix_ref[0]
    gain = gain_ref[0:1]
    sig = jax.nn.sigmoid(z)
    act = z * sig
    v = y * act * inv
    mixed_ref[0] = (v * gain).astype(BF16)
    d_gated = inv * (dmix * gain - v * mean_ev)
    dy = (d_gated * act).astype(BF16)
    dy_ref[0] = dy
    dz_ref[0] = (d_gated * y * sig * (1.0 + z * (1.0 - sig))).astype(BF16)
    part = jnp.sum(dmix * v, axis=0, keepdims=True)

    @pl.when(step == 0)
    def _():
        dgain_ref[...] = jnp.zeros_like(dgain_ref)

    dgain_ref[0:1] += part

    @pl.when(ctx_ref[0] != 0)
    def _():
        out_basis = xc_ref[0][:, HP + STATE :]
        enter = cols_ref[0][:, 3:4] * jnp.exp(cum_ref[0])
        left = lane_ids(LOCAL, 128) < HEAD_DIM
        for p in range(3):
            at = slice(128 * p, 128 * p + 128)
            part = (dy[:, at].astype(F32) * pair(enter, p, left)).astype(BF16)
            dstate_ref[0, at] = mm(part, out_basis, TN).astype(BF16)

    @pl.when(ctx_ref[0] == 0)
    def _():
        dstate_ref[0] = jnp.zeros((HP, STATE), BF16)


def back_scan_kernel_fn(
    ctx_ref, dy_ref, xc_ref, dt_ref, cum_ref, cols_ref, rows_ref, hp_ref, state_ref,
    dxs_ref, dbc_ref, dcum_ref, ddt_ref, dskip_ref, turn_ref,
):
    step = pl.program_id(0)
    xc = xc_ref[0]
    dy = dy_ref[0]
    dt = dt_ref[0]
    cum = cum_ref[0]
    hp = hp_ref[...]
    cum_t = cum.T
    dt_t = dt.T
    basis, out_basis = xc[:, HP : HP + STATE], xc[:, HP + STATE :]
    scores = mm(out_basis, basis, NT)
    bias = mask_bias(cols_ref[0], rows_ref[0])
    lane = lane_ids(LOCAL, 128)
    left = lane < HEAD_DIM
    left1 = lane_ids(1, 128) < HEAD_DIM

    @pl.when(step == 0)
    def _():
        dskip_ref[...] = jnp.zeros_like(dskip_ref)

    turn_ref[...] = jnp.zeros_like(turn_ref)
    d_scores = jnp.zeros((LOCAL, LOCAL), F32)
    row_sums = jnp.zeros((LOCAL, 128), F32)
    for p in range(3):
        at = slice(128 * p, 128 * p + 128)
        x = xc[:, at]
        g = dy[:, at]
        halves = []
        for h in (2 * p, 2 * p + 1):
            mine = left if h % 2 == 0 else ~left
            prod = mm(jnp.where(mine, g, jnp.zeros_like(g)), x, NT)
            mix = jnp.exp(cum[:, h : h + 1] - cum_t[h : h + 1] + bias)
            weighed = mix * prod
            d_scores = d_scores + weighed * dt_t[h : h + 1]
            kp = weighed * scores
            turn_ref[h : h + 1] = jnp.sum(kp, axis=0, keepdims=True)
            rows = jnp.sum(kp * dt_t[h : h + 1], axis=1, keepdims=True)
            row_sums = jnp.where(lane == h, rows, row_sums)
            halves.append(mm((mix * scores).astype(BF16), g, TN))
        gf = g.astype(F32)
        skip = pair(hp[2:3], p, left1)
        dxs_ref[0, :, at] = pair(dt, p, left) * jnp.where(left, halves[0], halves[1]) + skip * gf
        dskip_ref[0:1, at] += jnp.sum(gf * x.astype(F32), axis=0, keepdims=True)
    ddt = turn_ref[...].T
    ddt_ref[0] = ddt
    dcum_ref[0] = row_sums - dt * ddt
    low = d_scores.astype(BF16)
    dbc_ref[0, :, 0:STATE] = mm(low, out_basis, TN)
    dbc_ref[0, :, STATE:] = mm(low, basis, NN)

    @pl.when(ctx_ref[0] != 0)
    def _():
        enter = cols_ref[0][:, 3:4] * jnp.exp(cum)
        d_out = jnp.zeros((LOCAL, STATE), F32)
        extra = jnp.zeros((LOCAL, 128), F32)
        for p in range(3):
            at = slice(128 * p, 128 * p + 128)
            gate = pair(enter, p, left)
            state = state_ref[0, at]
            scaled = dy[:, at].astype(F32) * gate
            d_out = d_out + mm(scaled.astype(BF16), state, NN)
            both = scaled * mm(out_basis, state, NT)
            for h, mine in ((2 * p, left), (2 * p + 1, ~left)):
                total = jnp.sum(jnp.where(mine, both, 0.0), axis=1, keepdims=True)
                extra = jnp.where(lane == h, total, extra)
        dbc_ref[0, :, STATE:] += d_out
        dcum_ref[0] += extra


def back_conv_kernel_fn(
    ctx_ref, dxs_ref, dbc_ref, dcum_ref, ddt_ref, xc_ref, u_ref, xbc_ref, halo_ref, dt_ref,
    cum_ref, raw_ref, cols_ref, par_ref, hp_ref, dstate_ref,
    dxbc_ref, dhalo_ref, draw_ref, dpar_ref, dhead_ref, dxc_ref, dc_ref, dd_ref,
):
    step = pl.program_id(0)
    cols = cols_ref[0]
    par = par_ref[...]
    hp = hp_ref[...]
    dt = dt_ref[0]
    lane = lane_ids(LOCAL, 128)
    left = lane < HEAD_DIM
    dxc_ref[:, 0:HP] = dxs_ref[0]
    dxc_ref[:, HP:] = dbc_ref[0]
    dc_ref[...] = dcum_ref[0]
    dd_ref[...] = ddt_ref[0]

    @pl.when(step == 0)
    def _():
        dpar_ref[...] = jnp.zeros_like(dpar_ref)
        dhead_ref[...] = jnp.zeros_like(dhead_ref)

    @pl.when(ctx_ref[0] == 0)
    def _():
        cum = cum_ref[0]
        tail = cols[:, 4:5] * jnp.exp(cum[LOCAL - 1 : LOCAL] - cum)
        weight = tail * dt
        basis = xc_ref[0][:, HP : HP + STATE]
        d_basis = jnp.zeros((LOCAL, STATE), F32)
        d_weight = jnp.zeros((LOCAL, 128), F32)
        for p in range(3):
            at = slice(128 * p, 128 * p + 128)
            x = xc_ref[0][:, at].astype(F32)
            w = pair(weight, p, left)
            ds = dstate_ref[0, at]
            seen = mm(basis, ds, NT)
            dxc_ref[:, at] += w * seen
            d_basis = d_basis + mm((x * w).astype(BF16), ds, NN)
            both = x * seen
            for h, mine in ((2 * p, left), (2 * p + 1, ~left)):
                total = jnp.sum(jnp.where(mine, both, 0.0), axis=1, keepdims=True)
                d_weight = jnp.where(lane == h, total, d_weight)
        dxc_ref[:, HP : HP + STATE] += d_basis
        dd_ref[...] += tail * d_weight
        moved = weight * d_weight
        dc_ref[...] -= moved
        dc_ref[LOCAL - 1 : LOCAL] += jnp.sum(moved, axis=0, keepdims=True)

    d_decay = mm(triangle().astype(F32), dc_ref[...], TN, HIGH)
    rate = hp[1:2]
    d_raw = (dd_ref[...] + d_decay * rate) * jax.nn.sigmoid(raw_ref[0] + hp[0:1])
    draw_ref[0] = d_raw.astype(BF16)
    dhead_ref[0:1] += jnp.sum(d_decay * dt, axis=0, keepdims=True) * rate
    dhead_ref[1:2] += jnp.sum(d_raw, axis=0, keepdims=True)

    x = xbc_ref[0].astype(F32)
    halo = halo_ref[0]
    u = u_ref[0]
    sig = jax.nn.sigmoid(u)
    du = dxc_ref[...] * sig * (1.0 + u * (1.0 - sig))
    dpar_ref[4:5] += jnp.sum(du, axis=0, keepdims=True)
    dpar_ref[0:1] += jnp.sum(du * x, axis=0, keepdims=True)
    zeros = jnp.zeros((8, CH), F32)
    total = par[0:1] * du
    before = jnp.zeros((8, CH), F32)
    for k in range(1, 4):
        dpar_ref[k : k + 1] += jnp.sum(du * taps(x, halo, cols, k), axis=0, keepdims=True)
        ext = jnp.concatenate([zeros, du * cols[:, k - 1 : k] * par[k : k + 1], zeros], axis=0)
        total = total + ext[8 + k : 8 + k + LOCAL]
        before = before + ext[k : k + 8]
    dxbc_ref[0] = total.astype(BF16)
    dhalo_ref[0] = before


def spec(*shape):
    return shape


def call(fn, name, inputs, outputs, scratch=()):
    def block(shape, blocked):
        if blocked:
            rest = tuple(shape[1:])
            return pl.BlockSpec((1,) + rest, lambda i: (i,) + (0,) * len(rest))
        return pl.BlockSpec(tuple(shape), lambda i: (0,) * len(shape))

    in_specs = []
    for value, blocked in inputs:
        if value.ndim == 1:
            in_specs.append(pl.BlockSpec(memory_space=pltpu.SMEM))
        else:
            in_specs.append(block(value.shape, blocked))
    return pl.pallas_call(
        fn,
        name=name,
        grid=(GROUP,),
        in_specs=in_specs,
        out_specs=[block(shape, blocked) for shape, _, blocked in outputs],
        out_shape=[jax.ShapeDtypeStruct(shape, dtype) for shape, dtype, _ in outputs],
        scratch_shapes=list(scratch),
        compiler_params=pltpu.CompilerParams(
            dimension_semantics=("arbitrary",), vmem_limit_bytes=VMEM_LIMIT
        ),
    )(*[value for value, _ in inputs])


def place_kernel_fn(extra, where_ref, own_ref, sib_ref, out_ref):
    y = where_ref[0]
    core = where_ref[1]
    for mine, refs in ((0, (own_ref, sib_ref)), (1, (sib_ref, own_ref))):

        @pl.when(core == mine)
        def _(refs=refs):
            for c in range(2):
                for line in range(4):
                    slot = lax.rem(y - line + 4, 4)
                    block = refs[c][slot].astype(F32)
                    for a in range(2):
                        first = (2 * c + a) * 768 + 192 * line
                        out_ref[:, first : first + 192] = block[:, 192 * a : 192 * a + 192]
                if extra:
                    total = refs[c][0, :, HP:].astype(F32)
                    for slot in range(1, 4):
                        total = total + refs[c][slot, :, HP:].astype(F32)
                    out_ref[:, INNER + STATE * c : INNER + STATE * c + STATE] = total


def place(where, own, sib, columns):
    block = ROWS // 4
    width = own.shape[2]
    return pl.pallas_call(
        functools.partial(place_kernel_fn, columns > INNER),
        name="place_slabs",
        grid=(4,),
        in_specs=[
            pl.BlockSpec(memory_space=pltpu.SMEM),
            pl.BlockSpec((4, block, width), lambda i: (0, i, 0)),
            pl.BlockSpec((4, block, width), lambda i: (0, i, 0)),
        ],
        out_specs=pl.BlockSpec((block, columns), lambda i: (i, 0)),
        out_shape=jax.ShapeDtypeStruct((ROWS, columns), F32),
        compiler_params=pltpu.CompilerParams(
            dimension_semantics=("arbitrary",), vmem_limit_bytes=VMEM_LIMIT
        ),
    )(where, own, sib)


def dot(left, right, dims, dtype=F32):
    out = lax.dot_general(left, right, (dims, ((), ())), preferred_element_type=F32)
    return out.astype(dtype)


def per_device(
    tokens,
    segments,
    cotangent,
    gate_proj,
    mixer_proj,
    step_proj,
    final_proj,
    norm_gain,
    conv_kernel,
    conv_bias,
    step_offset,
    log_rates,
    skip_gain,
    gating_gain,
):
    ctx = lax.axis_index("ctx")
    x = lax.axis_index("fsdp")
    rep = lax.axis_index("rep")
    y, core = rep // 4, rep % 2
    flag = ctx.astype(jnp.int32).reshape(1)
    heads_at = [12 * (2 * core + a) + 3 * y for a in range(2)]

    def slab(values):
        wide = values.shape[-1] // HEADS
        parts = [
            lax.dynamic_slice_in_dim(values, at * wide, 3 * wide, axis=values.ndim - 1)
            for at in heads_at
        ]
        return jnp.concatenate(parts, axis=-1)

    def padded(values, width):
        return jnp.pad(values, [(0, 0)] * (values.ndim - 1) + [(0, width - values.shape[-1])])

    tokens_f = tokens.reshape(LOCAL, D).astype(F32)
    inv_rms = lax.rsqrt(jnp.mean(tokens_f * tokens_f, axis=1, keepdims=True) + EPS)
    normed = (tokens_f * inv_rms * norm_gain).astype(BF16)
    normed = lax.dynamic_slice_in_dim(
        jnp.concatenate([normed, normed], axis=1), ROWS * x, D, axis=1
    )
    own_seg = lax.dynamic_slice_in_dim(segments, ctx * LOCAL, LOCAL, axis=1)
    seg_row = padded(own_seg.astype(BF16), D)
    payload = jnp.concatenate([normed, jnp.pad(seg_row, ((0, 15), (0, 0)))], axis=0)

    def over_y(value):
        own, below, far, above = ring_gather(value, y_shift)
        mine = [own, below, far, above]
        return mine + [core_swap(part) for part in mine]

    token_parts = over_y(payload)
    normed_all = jnp.concatenate([part[:LOCAL] for part in token_parts], axis=0)
    seg_all = jnp.stack([part[LOCAL, :LOCAL] for part in token_parts]).astype(F32)

    x_part, bc_part = mixer_proj[:, :INNER], mixer_proj[:, INNER:]
    weight_x = jnp.concatenate([slab(x_part), bc_part, padded(slab(step_proj), 128)], axis=1)
    weight_z = slab(gate_proj)

    def over_x(value):
        own, below, far, above = ring_gather(value, x_shift)
        return jnp.concatenate([own, above, far, below], axis=0)

    full_x = over_x(weight_x)
    full_z = over_x(weight_z)
    w_xbc, w_step = full_x[:, :CH], full_x[:, CH:]

    rows_final = lax.dynamic_slice(final_proj, (192 * y, 768 * core), (192, 768))
    own, below, far, above = ring_gather(rows_final, x_shift)
    owners = jnp.stack([own, above, far, below])
    kept = rolled(owners, 2 * core - x + 4, 2).reshape(HP, 768)
    other = core_swap(rolled(owners, 2 - 2 * core - x + 4, 2)).reshape(HP, 768)
    w_final = jnp.where(
        core == 0, jnp.concatenate([kept, other], 1), jnp.concatenate([other, kept], 1)
    )

    cot = cotangent.reshape(LOCAL, D)
    cot_all = jnp.concatenate(over_y(cot), axis=0)

    seg = seg_all[:, :, None]
    shifted = [
        jnp.concatenate([seg[:, :k], seg[:, : LOCAL - k]], axis=1) == seg for k in range(1, 4)
    ]
    enter = (seg == seg[:, :1]) & (ctx == 1)
    tail = seg == seg[:, LOCAL - 1 :]
    cols = jnp.concatenate([m.astype(F32) for m in shifted + [enter, tail]] + [seg, seg, seg], -1)
    seg_rows = jnp.broadcast_to(seg_all[:, None, :], (GROUP, 8, LOCAL))
    par = jnp.concatenate(
        [slab(conv_kernel[:, :INNER]), conv_kernel[:, INNER:]], axis=1
    )
    bias = jnp.concatenate([slab(conv_bias[:INNER]), conv_bias[INNER:]])
    par = jnp.concatenate([par, bias[None], jnp.zeros((3, CH), F32)], axis=0)
    hp = jnp.stack([slab(step_offset), -jnp.exp(slab(log_rates)), slab(skip_gain)])
    hp = jnp.pad(hp, ((0, 5), (0, 128 - OWN)))
    gain = jnp.broadcast_to(slab(gating_gain)[None], (8, HP))

    def grouped(values):
        return values.reshape((GROUP, LOCAL) + values.shape[1:])

    xbc = grouped(dot(normed_all, w_xbc, NN, BF16))
    last = lax.ppermute(xbc[:, LOCAL - 3 :], "ctx", [(0, 1)])
    halo = jnp.pad(last.astype(F32), ((0, 0), (5, 0), (0, 0)))
    raw = grouped(dot(normed_all, w_step, NN))
    z = grouped(dot(normed_all, full_z, NN))

    token = (GROUP, LOCAL, 128)
    u, xc, dt, cum, state = call(
        conv_kernel_fn,
        "conv_states",
        [(flag, 0), (xbc, 1), (halo, 1), (raw, 1), (cols, 1), (par, 0), (hp, 0)],
        [
            ((GROUP, LOCAL, CH), F32, 1),
            ((GROUP, LOCAL, CH), BF16, 1),
            (token, F32, 1),
            (token, F32, 1),
            ((GROUP, HP, STATE), BF16, 1),
        ],
    )
    state_in = lax.ppermute(state, "ctx", [(0, 1)])
    dmix = grouped(dot(cot_all, w_final, NT))
    wide = (GROUP, LOCAL, HP)
    (y_local,) = call(
        scan_kernel_fn,
        "scan",
        [(xc, 1), (dt, 1), (cum, 1), (cols, 1), (seg_rows, 1), (hp, 0)],
        [(wide, F32, 1)],
    )
    y_all, sums = call(
        gate_kernel_fn,
        "gate",
        [
            (flag, 0), (y_local, 1), (state_in, 1), (z, 1), (dmix, 1), (xc, 1), (cum, 1),
            (cols, 1), (gain, 0),
        ],
        [(wide, F32, 1), ((GROUP, 8, LOCAL), F32, 1)],
    )

    swapped = core_swap(sums)
    sums = sums + jnp.concatenate([swapped[4:], swapped[:4]], axis=0)
    total = sums
    for steps in (1, 2, 3):
        got = y_shift(sums, steps).reshape(2, 4, 8, LOCAL)
        got = jnp.concatenate([got[:, 4 - steps :], got[:, : 4 - steps]], axis=1)
        total = total + got.reshape(GROUP, 8, LOCAL)

    mixed, dy, dz, dstate, dgain = call(
        ungate_kernel_fn,
        "ungate",
        [
            (flag, 0), (y_all, 1), (z, 1), (dmix, 1), (total, 1), (xc, 1), (cum, 1), (cols, 1),
            (gain, 0),
        ],
        [
            (wide, BF16, 1),
            (wide, BF16, 1),
            (wide, BF16, 1),
            ((GROUP, HP, STATE), BF16, 1),
            ((8, HP), F32, 0),
        ],
    )
    dstate_in = lax.ppermute(dstate, "ctx", [(1, 0)])

    def back_over_y(partial):
        mine, theirs = partial[: 4 * LOCAL], partial[4 * LOCAL :]
        both = (mine.astype(F32) + core_swap(theirs).astype(F32)).astype(BF16)
        blocks = both.reshape(4, LOCAL, D)
        return ring_scatter(blocks[0], blocks[3], blocks[2], blocks[1], y_shift)

    mixed_rows = mixed.reshape(GROUP * LOCAL, HP)
    layer_out = tokens_f + back_over_y(dot(mixed_rows, w_final, NN, BF16))

    g_final = dot(mixed_rows, cot_all, TN, BF16)
    kept = lax.dynamic_slice_in_dim(g_final, 768 * core, 768, axis=1).reshape(2, 192, 768)
    other = lax.dynamic_slice_in_dim(g_final, 768 - 768 * core, 768, axis=1)
    other = core_swap(other).reshape(2, 192, 768)
    owners = jnp.where(
        core == 0, jnp.concatenate([kept, other], 0), jnp.concatenate([other, kept], 0)
    )
    owners = rolled(owners, x, 4)
    piece = ring_scatter(owners[0], owners[1], owners[2], owners[3], x_shift).astype(BF16)
    piece = sum_z(piece)
    own, below, far, above = ring_gather(piece, y_shift)
    lines = rolled(jnp.stack([own, above, far, below]), 4 - y, 4)
    others = core_swap(lines)
    grad_final = jnp.where(
        core == 0, jnp.concatenate([lines, others], 2), jnp.concatenate([others, lines], 2)
    ).reshape(768, D).astype(F32)

    dxs, dbc, dcum, ddt, dskip = call(
        back_scan_kernel_fn,
        "back_scan",
        [
            (flag, 0), (dy, 1), (xc, 1), (dt, 1), (cum, 1), (cols, 1), (seg_rows, 1), (hp, 0),
            (state_in, 1),
        ],
        [
            (wide, F32, 1),
            ((GROUP, LOCAL, 2 * STATE), F32, 1),
            (token, F32, 1),
            (token, F32, 1),
            ((8, HP), F32, 0),
        ],
        [pltpu.VMEM((128, LOCAL), F32)],
    )
    dxbc, dhalo, draw, dpar, dhead = call(
        back_conv_kernel_fn,
        "back_conv",
        [
            (flag, 0), (dxs, 1), (dbc, 1), (dcum, 1), (ddt, 1), (xc, 1), (u, 1), (xbc, 1),
            (halo, 1), (dt, 1), (cum, 1), (raw, 1), (cols, 1), (par, 0), (hp, 0), (dstate_in, 1),
        ],
        [
            ((GROUP, LOCAL, CH), BF16, 1),
            ((GROUP, 8, CH), F32, 1),
            (token, BF16, 1),
            ((8, CH), F32, 0),
            ((8, 128), F32, 0),
        ],
        [
            pltpu.VMEM((LOCAL, CH), F32),
            pltpu.VMEM((LOCAL, 128), F32),
            pltpu.VMEM((LOCAL, 128), F32),
        ],
    )
    returned = lax.ppermute(dhalo[:, 5:].astype(BF16), "ctx", [(1, 0)])

    dz_rows = dz.reshape(GROUP * LOCAL, HP)
    g_gate = dot(normed_all, dz_rows, TN)
    d_normed = dot(dz_rows, full_z, NT)

    dxbc = jnp.concatenate(
        [
            dxbc[:, : LOCAL - 3],
            (dxbc[:, LOCAL - 3 :].astype(F32) + returned.astype(F32)).astype(BF16),
        ],
        axis=1,
    ).reshape(GROUP * LOCAL, CH)
    draw_rows = draw.reshape(GROUP * LOCAL, 128)
    d_normed = d_normed + dot(dxbc, w_xbc, NT) + dot(draw_rows, w_step, NT)
    d_normed = back_over_y(d_normed.astype(BF16))
    d_normed = lax.dynamic_slice_in_dim(
        jnp.concatenate([d_normed, d_normed], axis=1), D - ROWS * x, D, axis=1
    )
    w = tokens_f * inv_rms
    e1 = d_normed * norm_gain
    grad_tokens = cot.astype(F32) + inv_rms * (
        e1 - w * jnp.mean(e1 * w, axis=1, keepdims=True)
    )

    g_mixer = dot(normed_all, dxbc, TN)
    g_step = dot(draw_rows, normed_all, TN)
    norm_rows = (
        jnp.sum(g_gate * full_z.astype(F32), axis=1)
        + jnp.sum(g_mixer * w_xbc.astype(F32), axis=1)
        + jnp.sum(g_step.T * w_step.astype(F32), axis=1)
    )

    where = jnp.stack([y, core]).astype(jnp.int32)

    def slab_sum(slabs):
        blocks = slabs.reshape(4, ROWS, slabs.shape[1])
        piece = ring_scatter(blocks[0], blocks[1], blocks[2], blocks[3], x_shift)
        piece = sum_z(piece.astype(BF16))
        own, below, far, above = ring_gather(piece, y_shift)
        stack = jnp.stack([own, below, far, above])
        return stack, core_swap(stack)

    grad_gate = place(where, *slab_sum(g_gate.astype(BF16)), INNER)

    low = g_mixer.astype(BF16)
    parts = low[:, HP : HP + STATE], low[:, HP + STATE :]
    keep_bc = jnp.where(core == 0, parts[0], parts[1])
    send_bc = jnp.where(core == 0, parts[1], parts[0])
    low = jnp.concatenate([low[:, :HP], keep_bc + core_swap(send_bc)], axis=1)
    grad_mixer = place(where, *slab_sum(low), CONV_CH)

    top = jnp.concatenate([g_step[:OWN], norm_rows[None] / 1.0], axis=0)
    top = lax.dynamic_slice_in_dim(jnp.concatenate([top, top], axis=1), D - ROWS * x, D, axis=1)
    heads = jnp.sum(dskip[0].reshape(OWN, HEAD_DIM), axis=1)
    flat = jnp.concatenate(
        [dpar[:5].reshape(-1), dgain[0], heads, dhead[0, :OWN], dhead[1, :OWN]]
    )
    flat = jnp.pad(flat, (0, 9 * D - flat.shape[0])).reshape(9, D)
    small = jnp.concatenate([top, flat], axis=0)
    small = small + x_shift(small, 1) + x_shift(small, 2) + x_shift(small, 3)
    small = small + z_swap(small, 0)
    small = small + z_swap(small, 1)
    slots = jnp.stack([small, y_shift(small, -1), y_shift(small, 2), y_shift(small, 1)])
    lines = rolled(slots, 4 - y, 4)
    others = core_swap(lines)
    every = jnp.where(
        core == 0, jnp.stack([lines, others], 1), jnp.stack([others, lines], 1)
    )

    def whole(values):
        rows = values.shape[2]
        values = values.reshape(4, 2, rows, 2, -1)
        return values.transpose(2, 1, 3, 0, 4).reshape(rows, -1)

    mine = lax.dynamic_slice_in_dim(every[:, :, :OWN], ROWS * x, ROWS, axis=3)
    grad_step = whole(mine.transpose(0, 1, 3, 2))
    grad_norm = jnp.sum(every[:, :, OWN], axis=(0, 1)) / norm_gain
    flat = every[:, :, 7:].reshape(4, 2, 9 * D)
    conv = flat[:, :, : 5 * CH].reshape(4, 2, 5, CH)
    conv = jnp.concatenate([whole(conv[..., :HP]), jnp.sum(conv[..., HP:], axis=(0, 1))], axis=1)
    at = 5 * CH
    grad_gating = whole(flat[:, :, None, at : at + HP])[0]
    at += HP
    grad_skip, grad_rates, grad_offset = [
        whole(flat[:, :, None, at + OWN * i : at + OWN * i + OWN])[0] for i in range(3)
    ]
    shape = (1, LOCAL, D)
    return (
        layer_out.reshape(shape),
        grad_tokens.reshape(shape),
        grad_gate,
        grad_mixer,
        grad_step,
        grad_final,
        grad_norm,
        conv[:4],
        conv[4],
        grad_offset,
        grad_rates,
        grad_skip,
        grad_gating,
    )


def solution(mesh):
    tokens = P(("fsdp", "rep"), "ctx", None)
    rows = P("fsdp", None)
    return jax.shard_map(
        per_device,
        mesh=mesh,
        in_specs=(tokens, P(("fsdp", "rep"), None), tokens, rows, rows, rows, rows) + (P(),) * 7,
        out_specs=(tokens, tokens, rows, rows, rows, rows) + (P(),) * 7,
        check_vma=False,
    )
```

time: 1070 us -> 619 us (0.58)
  waiting for transfers between devices: 591 us -> 148 us
  blocking collectives: 149 us -> 0 us
  Pallas kernels: 0 us -> 92.5 us
  starting transfers between devices: 7.3 us -> 98.2 us
  matrix products: 169 us -> 93 us
  local copies, waits for them, and re-layouts: 65.7 us -> 106 us
  between operations: 18.2 us -> 2.43 us
  other arithmetic: 56 us -> 67.2 us
    all_gather x5 -> x0, waiting for transfers between devices: 255 us -> none  [the longest x1 84 us: per_device(): lax.all_gather(final_proj, 'fsdp', axis=0, tiled=True)]
    reduce_scatter x3 -> x0, waiting for transfers between devices: 198 us -> none  [the longest x1 97.6 us: per_device(): lax.psum_scatter(grad_mixer.astype(jnp.bfloat16), 'fsdp', scatter_dimensi...]
    ppermute x2 -> x91, waiting for transfers between devices: 6.94 us -> 148 us  [the longest x34 82.5 us: y_shift(): return lax.ppermute(value, 'rep', pairs)]
    psum x1 -> x0, blocking collectives: 129 us -> none  [per_device(): lax.psum(owned[2].astype(jnp.bfloat16), ('ctx', 'rep')).astype(jnp.float32)]
    psum x2 -> x0, waiting for transfers between devices: 128 us -> none  [the longest x1 128 us: per_device(): lax.psum((d_norm, d_kernel, d_bias, d_offset_a + d_offset_b, d_rates_a +...]
    pallas_call x0 -> x8, Pallas kernels: none -> 92.5 us  [the longest x6 82.9 us: call(): pl.pallas_call(fn, name=name, grid=(GROUP,), in_specs=in_specs, out_specs...]
    ppermute x2 -> x91, starting transfers between devices: 6.61 us -> 98.2 us  [the longest x34 39.9 us: y_shift(): return lax.ppermute(value, 'rep', pairs)]
    dot_general x26 -> x12, matrix products: 169 us -> 93 us  [dot(): lax.dot_general(left, right, (dims, ((), ())), preferred_element_type=F32)]
  transfers between devices with their start and end apart: 13 -> 91, of which waited for: 10 -> 32; matrix products, arithmetic and copies ran while one was open for 21% -> 37% of each run, Pallas kernels for 0% -> 12%
where the time goes in v1:
time: 619 us; the launch traced here: 607 us
  waiting for transfers between devices  148 us (24%)
  local copies, waits for them, and re-layouts  106 us (17%)
  starting transfers between devices  98.2 us (16%)
  matrix products  93 us (15%)
  Pallas kernels  92.5 us (15%)
  other arithmetic  67.2 us (11%)
    dot_general x12, matrix products, dot(): lax.dot_general(left, right, (dims, ((), ())), preferred_element_type=F32)  93 us
    pallas_call x6, Pallas kernels, call(): pl.pallas_call(fn, name=name, grid=(GROUP,), in_specs=in_specs, out_specs...  82.9 us
    ppermute x34, waiting for transfers between devices, y_shift(): return lax.ppermute(value, 'rep', pairs)  82.5 us
    ppermute x34, starting transfers between devices, y_shift(): return lax.ppermute(value, 'rep', pairs)  39.9 us
    ppermute x27, starting transfers between devices, x_shift(): return lax.ppermute(value, 'fsdp', [(i, (i + steps) % 4) for i in range(4)])  35.7 us
    ppermute x27, waiting for transfers between devices, x_shift(): return lax.ppermute(value, 'fsdp', [(i, (i + steps) % 4) for i in range(4)])  33 us
    unnamed x158, local copies, waits for them, and re-layouts  31.1 us
    ppermute x4, waiting for transfers between devices, z_swap(): return lax.ppermute(value, 'ctx', [(0, 1), (1, 0)])  17.2 us
  transfers between devices with their start and end apart: 91, of which 32 were waited for; matrix products, arithmetic and copies ran while one was open for 37% of the time, Pallas kernels for 12%

profile of v1, /device:TPU:0, one launch (start us, length us, event | category | flops | bytes accessed | tf_op | source)
XLA Modules:
  0.0 607.3 jit_solution(7582567344687607230)
XLA Ops:
  41.2 8.9 %collective-permute-done.16 = bf16[192,384]{1,0:T(8,128)(2,1)S(1)} collective-permute-done((bf16[192,384]{1,0:T(8,128)(2,1)S(1)}, bf16[192,384]{1,0:T(8,128)(2,1)S(1)}, u32[]{:S(2)}, u32[]{:S(2)}) %collective-permute-start.16) | collective-permute-done | bytes 147488 | tf_op jit(solution)/shard_map/ppermute | solution.py:31
  73.8 10.2 %collective-permute-done.2 = bf16[272,1536]{1,0:T(8,128)(2,1)S(1)} collective-permute-done((bf16[272,1536]{1,0:T(8,128)(2,1)S(1)}, bf16[272,1536]{1,0:T(8,128)(2,1)S(1)}, u32[]{:S(2)}, u32[]{:S(2)}) %collective-permute-start.2) | collective-permute-done | bytes 835616 | tf_op jit(solution)/shard_map/ppermute | solution.py:36
  132.0 9.2 %convolution_convert_fusion.1 = bf16[2048,640]{1,0:T(8,128)(2,1)} fusion(bf16[2048,1536]{1,0:T(8,128)(2,1)} %slice_dynamic-update-slice_fusion, bf16[1536,768]{0,1:T(8,128)(2,1)S(1)} %copy-done.4), kind=kOutput, calls=%fused_computation.11 | convolution fusion | flops 4027842560 | bytes 10878976 | tf_op jit(solution)/shard_map/dot_general | solution.py:455
  159.1 6.2 %concatenate.262.cols_ref = f32[8,256,8]{2,1,0:T(8,128)} concatenate(f32[8,256,1]{2,1,0:T(8,128)} %get-tuple-element.103, f32[8,256,1]{2,1,0:T(8,128)} %get-tuple-element.102, f32[8,256,1]{2,1,0:T(8,128)S(1)} %get-tuple-element.101, f32[8,256,1]{2,1,0:T(8,128)} %and_convert_fusion, f32[8,256,1]{2,1,0:T(8,128)} %copy.200, f32[8,256,1]{2,1,0:T(8,128)S(1)} %copy.190, ...), dimensions={2} | concatenate | bytes 131072 | tf_op jit(solution)/shard_map/concatenate | solution.py:542
  165.9 14.2 %conv_states.1 = (f32[8,256,640]{2,1,0:T(8,128)}, bf16[8,256,640]{2,1,0:T(8,128)(2,1)}, f32[8,256,128]{2,1,0:T(8,128)}, f32[8,256,128]{2,1,0:T(8,128)}, bf16[8,384,128]{2,1,0:T(8,128)(2,1)}) custom-call(s32[1]{0:T(128)} %bitcast.1.ctx_ref, bf16[8,256,640]{2,1,0:T(8,128)(2,1)} %bitcast.217, f32[8,8,640]{2,1,0:T(8,128)} %pad_convert_fusion.halo_ref, ...), custom_call_target="tpu_custom_call" | custom-call | tf_op jit(solution)/shard_map/conv_states/pallas_call | solution.py:399
  181.9 8.2 %fusion.32 = f32[2048,384]{1,0:T(8,128)} fusion(bf16[2048,1536]{1,0:T(8,128)(2,1)} %constant_dynamic-update-slice_fusion.8, bf16[384,768]{1,0:T(8,128)(2,1)} %bitcast.32, bf16[384,768]{1,0:T(8,128)(2,1)S(1)} %bitcast.239, pred[]{:T(512)S(6)} %eq.97), kind=kOutput, calls=%fused_computation.119 | convolution fusion | flops 2421227520 | bytes 10616833 | tf_op jit(solution)/shard_map/dot_general | solution.py:455
  190.2 8.2 %fusion.73 = f32[2048,384]{1,0:T(8,128)} fusion(bf16[2048,1536]{1,0:T(8,128)(2,1)} %slice_dynamic-update-slice_fusion, bf16[1536,384]{1,0:T(8,128)(2,1)} %constant_dynamic-update-slice_fusion.3), kind=kOutput, calls=%fused_computation.264 | convolution fusion | flops 2415919104 | bytes 10616832 | tf_op jit(solution)/shard_map/dot_general | solution.py:455
  199.0 10.0 %scan.1.y_ref = f32[8,256,384]{2,1,0:T(8,128)} custom-call(bf16[8,256,640]{2,1,0:T(8,128)(2,1)} %get-tuple-element.35.xc_ref, f32[8,256,128]{2,1,0:T(8,128)} %get-tuple-element.36.dt_ref, f32[8,256,128]{2,1,0:T(8,128)} %get-tuple-element.37.cum_ref, f32[8,256,8]{2,1,0:T(8,128)} %concatenate.262.cols_ref, f32[8,8,256]{2,1,0:T(8,128)} %broadcast_in_dim.10.rows_ref, ...), custom_call_target="tpu_custom_call" | custom-call | tf_op jit(solution)/shard_map/scan/pallas_call | solution.py:399
  209.9 8.8 %gate.1 = (f32[8,256,384]{2,1,0:T(8,128)}, f32[8,8,256]{2,1,0:T(8,128)}) custom-call(s32[1]{0:T(128)} %bitcast.1.ctx_ref, f32[8,256,384]{2,1,0:T(8,128)} %scan.1.y_ref, bf16[8,384,128]{2,1,0:T(8,128)(2,1)} %copy-done.7, f32[8,256,384]{2,1,0:T(8,128)} %bitcast.214, f32[8,256,384]{2,1,0:T(8,128)} %bitcast.212, bf16[8,256,640]{2,1,0:T(8,128)(2,1)} %get-tuple-element.35.xc_ref, ...), custom_call_target="tpu_custom_call" | custom-call | tf_op jit(solution)/shard_map/gate/pallas_call | solution.py:399
  232.3 11.0 %ungate.1 = (bf16[8,256,384]{2,1,0:T(8,128)(2,1)}, bf16[8,256,384]{2,1,0:T(8,128)(2,1)}, bf16[8,256,384]{2,1,0:T(8,128)(2,1)}, bf16[8,384,128]{2,1,0:T(8,128)(2,1)}, f32[8,384]{1,0:T(8,128)}) custom-call(s32[1]{0:T(128)} %bitcast.1.ctx_ref, f32[8,256,384]{2,1,0:T(8,128)} %get-tuple-element.39.y_ref, f32[8,256,384]{2,1,0:T(8,128)} %bitcast.215, ...), custom_call_target="tpu_custom_call" | custom-call | tf_op jit(solution)/shard_map/ungate/pallas_call | solution.py:399
  254.4 9.5 %multiply_reduce_fusion.1 = (f32[1536]{0:T(1024)}, bf16[1536,384]{1,0:T(8,128)(2,1)S(1)}) fusion(bf16[1536,384]{1,0:T(8,128)(2,1)} %constant_dynamic-update-slice_fusion.3, bf16[2048,1536]{1,0:T(8,128)(2,1)} %slice_dynamic-update-slice_fusion, bf16[2048,384]{1,0:T(8,128)(2,1)S(1)} %bitcast.231), kind=kOutput, calls=%fused_computation.23 | convolution fusion | flops 2418276864 | bytes 10229760 | tf_op jit(solution)/shard_map/dot_general | solution.py:455
  263.9 8.1 %fusion.74 = f32[2048,1536]{1,0:T(8,128)} fusion(bf16[2048,384]{1,0:T(8,128)(2,1)S(1)} %bitcast.232, bf16[1536,384]{1,0:T(8,128)(2,1)} %constant_dynamic-update-slice_fusion.3), kind=kOutput, calls=%fused_computation.265 | convolution fusion | flops 2415919104 | bytes 15335424 | tf_op jit(solution)/shard_map/dot_general | solution.py:455
  276.9 19.0 %back_scan.1 = (f32[8,256,384]{2,1,0:T(8,128)}, f32[8,256,256]{2,1,0:T(8,128)}, f32[8,256,128]{2,1,0:T(8,128)}, f32[8,256,128]{2,1,0:T(8,128)}, f32[8,384]{1,0:T(8,128)}) custom-call(s32[1]{0:T(128)} %bitcast.1.ctx_ref, bf16[8,256,384]{2,1,0:T(8,128)(2,1)} %get-tuple-element.43.dy_ref, bf16[8,256,640]{2,1,0:T(8,128)(2,1)} %get-tuple-element.35.xc_ref, ...), custom_call_target="tpu_custom_call" | custom-call | tf_op jit(solution)/shard_map/back_scan/pallas_call | solution.py:399
  320.1 19.8 %back_conv.1 = (bf16[8,256,640]{2,1,0:T(8,128)(2,1)}, f32[8,8,640]{2,1,0:T(8,128)}, bf16[8,256,128]{2,1,0:T(8,128)(2,1)}, f32[8,640]{1,0:T(8,128)}, f32[8,128]{1,0:T(8,128)}) custom-call(s32[1]{0:T(128)} %bitcast.1.ctx_ref, f32[8,256,384]{2,1,0:T(8,128)} %get-tuple-element.44.dxs_ref, f32[8,256,256]{2,1,0:T(8,128)} %get-tuple-element.45.dbc_ref, ...), custom_call_target="tpu_custom_call" | custom-call | tf_op jit(solution)/shard_map/back_conv/pallas_call | solution.py:399
  355.3 8.6 %multiply_reduce_fusion = (f32[1536]{0:T(1024)S(1)}, bf16[1536,640]{0,1:T(8,128)(2,1)}) fusion(bf16[1536,768]{0,1:T(8,128)(2,1)S(1)} %copy-done.5, bf16[2048,1536]{1,0:T(8,128)(2,1)} %slice_dynamic-update-slice_fusion, bf16[2048,640]{1,0:T(8,128)(2,1)S(1)} %bitcast.226), kind=kOutput, calls=%fused_computation.4 | convolution fusion | flops 4030462464 | bytes 12851200 | tf_op jit(solution)/shard_map/dot_general | solution.py:455
  368.7 8.4 %fusion.15 = f32[2048,1536]{1,0:T(8,128)} fusion(bf16[2048,640]{1,0:T(8,128)(2,1)S(1)} %bitcast.227, bf16[1536,768]{0,1:T(8,128)(2,1)S(1)} %copy-done.5), kind=kOutput, calls=%fused_computation.49 | convolution fusion | flops 4026531840 | bytes 17170432 | tf_op jit(solution)/shard_map/dot_general | solution.py:455
  379.8 12.1 %add_convert_fusion = bf16[2048,1536]{1,0:T(8,128)(2,1)} fusion(f32[2048,1536]{1,0:T(8,128)} %fusion.74, f32[2048,1536]{1,0:T(8,128)} %fusion.15, bf16[2048,128]{1,0:T(8,128)(2,1)S(1)} %bitcast.230, bf16[1536,768]{0,1:T(8,128)(2,1)S(1)} %copy-done.5), kind=kOutput, calls=%fused_computation | convolution fusion | flops 814743552 | bytes 32374784 | tf_op jit(solution)/shard_map/dot_general | solution.py:455
  409.9 8.4 %collective-permute-done.52 = bf16[384,384]{1,0:T(8,128)(2,1)S(1)} collective-permute-done((bf16[384,384]{1,0:T(8,128)(2,1)S(1)}, bf16[384,384]{1,0:T(8,128)(2,1)S(1)}, u32[]{:S(2)}, u32[]{:S(2)}) %collective-permute-start.52) | collective-permute-done | bytes 294944 | tf_op jit(solution)/shard_map/ppermute | solution.py:46
  434.7 7.0 %collective-permute-done.59 = bf16[192,512]{1,0:T(8,128)(2,1)S(1)} collective-permute-done((bf16[192,512]{1,0:T(8,128)(2,1)S(1)}, bf16[192,512]{1,0:T(8,128)(2,1)S(1)}, u32[]{:S(2)}, u32[]{:S(2)}) %collective-permute-start.59) | collective-permute-done | bytes 196640 | tf_op jit(solution)/shard_map/ppermute | solution.py:31
  501.6 9.7 %collective-permute-done.63 = bf16[384,512]{1,0:T(8,128)(2,1)S(1)} collective-permute-done((bf16[384,512]{1,0:T(8,128)(2,1)S(1)}, bf16[384,512]{1,0:T(8,128)(2,1)S(1)}, u32[]{:S(2)}, u32[]{:S(2)}) %collective-permute-start.63) | collective-permute-done | bytes 393248 | tf_op jit(solution)/shard_map/ppermute | solution.py:45
  511.9 8.8 %collective-permute-done.64 = bf16[384,512]{1,0:T(8,128)(2,1)S(1)} collective-permute-done((bf16[384,512]{1,0:T(8,128)(2,1)S(1)}, bf16[384,512]{1,0:T(8,128)(2,1)S(1)}, u32[]{:S(2)}, u32[]{:S(2)}) %collective-permute-start.64) | collective-permute-done | bytes 393248 | tf_op jit(solution)/shard_map/ppermute | solution.py:46
  555.4 8.8 %collective-permute-done.45 = bf16[128,1536]{1,0:T(8,128)(2,1)S(1)} collective-permute-done((bf16[128,1536]{1,0:T(8,128)(2,1)S(1)}, bf16[128,1536]{1,0:T(8,128)(2,1)S(1)}, u32[]{:S(2)}, u32[]{:S(2)}) %collective-permute-start.45) | collective-permute-done | bytes 393248 | tf_op jit(solution)/shard_map/ppermute | solution.py:36
  580.9 8.7 %collective-permute-done.46 = bf16[256,1536]{1,0:T(8,128)(2,1)} collective-permute-done((bf16[256,1536]{1,0:T(8,128)(2,1)}, bf16[256,1536]{1,0:T(8,128)(2,1)}, u32[]{:S(2)}, u32[]{:S(2)}) %collective-permute-start.46) | collective-permute-done | bytes 786464 | tf_op jit(solution)/shard_map/ppermute | solution.py:36
  592.1 10.9 %collective-permute-done.39 = bf16[256,1536]{1,0:T(8,128)(2,1)} collective-permute-done((bf16[256,1536]{1,0:T(8,128)(2,1)}, bf16[256,1536]{1,0:T(8,128)(2,1)}, u32[]{:S(2)}, u32[]{:S(2)}) %collective-permute-start.39) | collective-permute-done | bytes 786464 | tf_op jit(solution)/shard_map/ppermute | solution.py:36
  (561 shorter events, 362.0 us)
Async XLA Ops:
  5.4 26.0 %collective-permute-start.14 = (bf16[384,384]{1,0:T(8,128)(2,1)}, bf16[384,384]{1,0:T(8,128)(2,1)}, u32[]{:S(2)}, u32[]{:S(2)}) collective-permute-start(bf16[384,384]{1,0:T(8,128)(2,1)} %get-tuple-element.64), channel_id=1, source_target_pairs={{0,48},{16,0},{32,16},{48,32},{1,49},{17,1},{33,17},{49,33},{2,50}... | collective-permute-start | bytes 884744 | tf_op jit(solution)/shard_map/ppermute | solution.py:31
  13.3 53.9 %collective-permute-start.20 = (bf16[256,1536]{1,0:T(8,128)(2,1)S(1)}, bf16[256,1536]{1,0:T(8,128)(2,1)}, u32[]{:S(2)}, u32[]{:S(2)}) collective-permute-start(bf16[256,1536]{1,0:T(8,128)(2,1)S(1)} %bitcast.222), channel_id=1, source_target_pairs={{0,12},{1,13},{2,14},{3,15},{4,0},{5,1},{6,2},{7,3},{8,4},{9,5},{1... | collective-permute-start | bytes 2359304 | tf_op jit(solution)/shard_map/ppermute | solution.py:36
  31.4 31.3 %collective-permute-start.18 = (bf16[256,1536]{1,0:T(8,128)(2,1)S(1)}, bf16[256,1536]{1,0:T(8,128)(2,1)S(1)}, u32[]{:S(2)}, u32[]{:S(2)}) collective-permute-start(bf16[256,1536]{1,0:T(8,128)(2,1)S(1)} %bitcast.223), channel_id=1, source_target_pairs={{0,4},{1,5},{2,6},{3,7},{4,8},{5,9},{6,10},{7,11},{8,12},{9,13},{1... | collective-permute-start | bytes 2359304 | tf_op jit(solution)/shard_map/ppermute | solution.py:36
  32.3 24.9 %collective-permute-start.9 = (bf16[384,768]{0,1:T(8,128)(2,1)S(1)}, bf16[384,768]{0,1:T(8,128)(2,1)S(1)}, u32[]{:S(2)}, u32[]{:S(2)}) collective-permute-start(bf16[384,768]{0,1:T(8,128)(2,1)S(1)} %pad_maximum_fusion.8), channel_id=1, source_target_pairs={{0,16},{16,32},{32,48},{48,0},{1,17},{17,33},{33,49},{49,1},{2,18}... | collective-permute-start | bytes 1769480 | tf_op jit(solution)/shard_map/ppermute | solution.py:31
  57.3 46.1 %collective-permute-start.22 = (bf16[256,1536]{1,0:T(8,128)(2,1)S(1)}, bf16[256,1536]{1,0:T(8,128)(2,1)}, u32[]{:S(2)}, u32[]{:S(2)}) collective-permute-start(bf16[256,1536]{1,0:T(8,128)(2,1)S(1)} %bitcast.224), channel_id=1, source_target_pairs={{0,1},{1,0},{2,3},{3,2},{4,5},{5,4},{6,7},{7,6},{8,9},{9,8},{10,11... | collective-permute-start | bytes 2359304 | tf_op jit(solution)/shard_map/ppermute | solution.py:40
  90.5 91.4 %collective-permute-start.30 = (bf16[2,192,768]{2,1,0:T(8,128)(2,1)}, bf16[2,192,768]{2,1,0:T(8,128)(2,1)}, u32[]{:S(2)}, u32[]{:S(2)}) collective-permute-start(bf16[2,192,768]{2,1,0:T(8,128)(2,1)} %get-tuple-element.78), channel_id=1, source_target_pairs={{0,1},{1,0},{2,3},{3,2},{4,5},{5,4},{6,7},{7,6},{8,9},{9,8},{10,11... | collective-permute-start | bytes 1769480 | tf_op jit(solution)/shard_map/ppermute | solution.py:40
  90.5 29.3 %collective-permute-start.25 = (bf16[256,1536]{1,0:T(8,128)(2,1)}, bf16[256,1536]{1,0:T(8,128)(2,1)}, u32[]{:S(2)}, u32[]{:S(2)}) collective-permute-start(bf16[256,1536]{1,0:T(8,128)(2,1)} %collective-permute-done.20), channel_id=1, source_target_pairs={{0,1},{1,0},{2,3},{3,2},{4,5},{5,4},{6,7},{7,6},{8,9},{9,8},{10,11... | collective-permute-start | bytes 2359304 | tf_op jit(solution)/shard_map/ppermute | solution.py:40
  180.1 28.8 %collective-permute-start.13 = (bf16[8,384,128]{2,1,0:T(8,128)(2,1)}, bf16[8,384,128]{2,1,0:T(8,128)(2,1)S(1)}, u32[]{:S(2)}, u32[]{:S(2)}) collective-permute-start(bf16[8,384,128]{2,1,0:T(8,128)(2,1)} %get-tuple-element.38), channel_id=1, source_target_pairs={{0,64},{1,65},{2,66},{3,67},{4,68},{5,69},{6,70},{7,71},{8,72},{9,... | collective-permute-start | bytes 2359304 | tf_op jit(solution)/shard_map/ppermute | solution.py:575
  272.1 24.6 %collective-permute-start.47 = (bf16[192,384]{1,0:T(8,128)(2,1)S(1)}, bf16[192,384]{1,0:T(8,128)(2,1)S(1)}, u32[]{:S(2)}, u32[]{:S(2)}) collective-permute-start(bf16[192,384]{1,0:T(8,128)(2,1)S(1)} %slice.632), channel_id=1, source_target_pairs={{0,16},{16,32},{32,48},{48,0},{1,17},{17,33},{33,49},{49,1},{2,18}... | collective-permute-start | bytes 442376 | tf_op jit(solution)/shard_map/ppermute | solution.py:31
  273.1 36.0 %collective-permute-start.79 = (bf16[384,768]{1,0:T(8,128)(2,1)}, bf16[384,768]{1,0:T(8,128)(2,1)S(1)}, u32[]{:S(2)}, u32[]{:S(2)}) collective-permute-start(bf16[384,768]{1,0:T(8,128)(2,1)} %get-tuple-element.94), channel_id=1, source_target_pairs={{0,1},{1,0},{2,3},{3,2},{4,5},{5,4},{6,7},{7,6},{8,9},{9,8},{10,11... | collective-permute-start | bytes 1769480 | tf_op jit(solution)/shard_map/ppermute | solution.py:40
  273.1 47.1 %collective-permute-start.40 = (bf16[8,384,128]{2,1,0:T(8,128)(2,1)}, bf16[8,384,128]{2,1,0:T(8,128)(2,1)}, u32[]{:S(2)}, u32[]{:S(2)}) collective-permute-start(bf16[8,384,128]{2,1,0:T(8,128)(2,1)} %get-tuple-element.49), channel_id=1, source_target_pairs={{64,0},{65,1},{66,2},{67,3},{68,4},{69,5},{70,6},{71,7},{72,8},{73... | collective-permute-start | bytes 2359304 | tf_op jit(solution)/shard_map/ppermute | solution.py:617
  276.2 252.4 %collective-permute-start.35 = (bf16[1024,1536]{1,0:T(8,128)(2,1)}, bf16[1024,1536]{1,0:T(8,128)(2,1)}, u32[]{:S(2)}, u32[]{:S(2)}) collective-permute-start(bf16[1024,1536]{1,0:T(8,128)(2,1)} %slice.612), channel_id=1, source_target_pairs={{0,1},{1,0},{2,3},{3,2},{4,5},{5,4},{6,7},{7,6},{8,9},{9,8},{10,11... | collective-permute-start | bytes 9437192 | tf_op jit(solution)/shard_map/ppermute | solution.py:40
  317.3 89.0 %collective-permute-start.51 = (bf16[384,384]{1,0:T(8,128)(2,1)S(1)}, bf16[384,384]{1,0:T(8,128)(2,1)}, u32[]{:S(2)}, u32[]{:S(2)}) collective-permute-start(bf16[384,384]{1,0:T(8,128)(2,1)S(1)} %add_convert_fusion.4), channel_id=1, source_target_pairs={{0,2},{1,3},{2,0},{3,1},{4,6},{5,7},{6,4},{7,5},{8,10},{9,11},{10,... | collective-permute-start | bytes 884744 | tf_op jit(solution)/shard_map/ppermute | solution.py:45
  377.2 30.3 %collective-permute-start.83 = (bf16[192,768]{1,0:T(8,128)(2,1)}, bf16[192,768]{1,0:T(8,128)(2,1)}, u32[]{:S(2)}, u32[]{:S(2)}) collective-permute-start(bf16[192,768]{1,0:T(8,128)(2,1)} %pad_maximum_fusion.15), channel_id=1, source_target_pairs={{0,48},{16,0},{32,16},{48,32},{1,49},{17,1},{33,17},{49,33},{2,50}... | collective-permute-start | bytes 884744 | tf_op jit(solution)/shard_map/ppermute | solution.py:31
  379.6 28.4 %collective-permute-start.81 = (bf16[192,768]{1,0:T(8,128)(2,1)}, bf16[192,768]{1,0:T(8,128)(2,1)}, u32[]{:S(2)}, u32[]{:S(2)}) collective-permute-start(bf16[192,768]{1,0:T(8,128)(2,1)} %pad_maximum_fusion.14), channel_id=1, source_target_pairs={{0,16},{16,32},{32,48},{48,0},{1,17},{17,33},{33,49},{49,1},{2,18}... | collective-permute-start | bytes 884744 | tf_op jit(solution)/shard_map/ppermute | solution.py:31
  406.3 25.4 %collective-permute-start.58 = (bf16[1536,128]{1,0:T(8,128)(2,1)S(1)}, bf16[1536,128]{1,0:T(8,128)(2,1)S(1)}, u32[]{:S(2)}, u32[]{:S(2)}) collective-permute-start(bf16[1536,128]{1,0:T(8,128)(2,1)S(1)} %broadcast_select_fusion), channel_id=1, source_target_pairs={{0,1},{1,0},{2,3},{3,2},{4,5},{5,4},{6,7},{7,6},{8,9},{9,8},{10,11... | collective-permute-start | bytes 1179656 | tf_op jit(solution)/shard_map/ppermute | solution.py:40
  407.4 129.6 %collective-permute-start.42 = (bf16[1024,1536]{1,0:T(8,128)(2,1)}, bf16[1024,1536]{1,0:T(8,128)(2,1)}, u32[]{:S(2)}, u32[]{:S(2)}) collective-permute-start(bf16[1024,1536]{1,0:T(8,128)(2,1)} %slice.622), channel_id=1, source_target_pairs={{0,1},{1,0},{2,3},{3,2},{4,5},{5,4},{6,7},{7,6},{8,9},{9,8},{10,11... | collective-permute-start | bytes 9437192 | tf_op jit(solution)/shard_map/ppermute | solution.py:40
  443.8 26.6 %collective-permute-start.85 = (bf16[192,768]{1,0:T(8,128)(2,1)S(1)}, bf16[192,768]{1,0:T(8,128)(2,1)}, u32[]{:S(2)}, u32[]{:S(2)}) collective-permute-start(bf16[192,768]{1,0:T(8,128)(2,1)S(1)} %add.344), channel_id=1, source_target_pairs={{0,64},{64,0},{1,65},{65,1},{2,66},{66,2},{3,67},{67,3},{4,68},{68... | collective-permute-start | bytes 884744 | tf_op jit(solution)/shard_map/ppermute | solution.py:46
  488.9 32.0 %collective-permute-start.57 = (bf16[4,384,384]{2,1,0:T(8,128)(2,1)S(1)}, bf16[4,384,384]{2,1,0:T(8,128)(2,1)S(1)}, u32[]{:S(2)}, u32[]{:S(2)}) collective-permute-start(bf16[4,384,384]{2,1,0:T(8,128)(2,1)S(1)} %pad_maximum_fusion.2.own_ref), channel_id=1, source_target_pairs={{0,1},{1,0},{2,3},{3,2},{4,5},{5,4},{6,7},{7,6},{8,9},{9,8},{10,11... | collective-permute-start | bytes 3538952 | tf_op jit(solution)/shard_map/ppermute | solution.py:40
  511.6 28.3 %collective-permute-start.90 = (bf16[4,192,768]{2,1,0:T(8,128)(2,1)S(1)}, bf16[4,192,768]{2,1,0:T(8,128)(2,1)}, u32[]{:S(2)}, u32[]{:S(2)}) collective-permute-start(bf16[4,192,768]{2,1,0:T(8,128)(2,1)S(1)} %constant_dynamic-slice_fusion), channel_id=1, source_target_pairs={{0,1},{1,0},{2,3},{3,2},{4,5},{5,4},{6,7},{7,6},{8,9},{9,8},{10,11... | collective-permute-start | bytes 3538952 | tf_op jit(solution)/shard_map/ppermute | solution.py:40
  549.0 25.8 %collective-permute-start.69 = (bf16[4,384,512]{2,1,0:T(8,128)(2,1)S(1)}, bf16[4,384,512]{2,1,0:T(8,128)(2,1)S(1)}, u32[]{:S(2)}, u32[]{:S(2)}) collective-permute-start(bf16[4,384,512]{2,1,0:T(8,128)(2,1)S(1)} %pad_maximum_fusion.1.own_ref), channel_id=1, source_target_pairs={{0,1},{1,0},{2,3},{3,2},{4,5},{5,4},{6,7},{7,6},{8,9},{9,8},{10,11... | collective-permute-start | bytes 4718600 | tf_op jit(solution)/shard_map/ppermute | solution.py:40
  554.2 26.7 %collective-permute-start.44 = (bf16[256,1536]{1,0:T(8,128)(2,1)}, bf16[256,1536]{1,0:T(8,128)(2,1)}, u32[]{:S(2)}, u32[]{:S(2)}) collective-permute-start(bf16[256,1536]{1,0:T(8,128)(2,1)} %pad_maximum_fusion.6), channel_id=1, source_target_pairs={{0,4},{1,5},{2,6},{3,7},{4,8},{5,9},{6,10},{7,11},{8,12},{9,13},{1... | collective-permute-start | bytes 2359304 | tf_op jit(solution)/shard_map/ppermute | solution.py:36
  567.4 24.7 %collective-permute-start.37 = (bf16[256,1536]{1,0:T(8,128)(2,1)}, bf16[256,1536]{1,0:T(8,128)(2,1)}, u32[]{:S(2)}, u32[]{:S(2)}) collective-permute-start(bf16[256,1536]{1,0:T(8,128)(2,1)} %pad_maximum_fusion.4), channel_id=1, source_target_pairs={{0,4},{1,5},{2,6},{3,7},{4,8},{5,9},{6,10},{7,11},{8,12},{9,13},{1... | collective-permute-start | bytes 2359304 | tf_op jit(solution)/shard_map/ppermute | solution.py:36
  573.6 29.4 %collective-permute-start.39 = (bf16[256,1536]{1,0:T(8,128)(2,1)}, bf16[256,1536]{1,0:T(8,128)(2,1)}, u32[]{:S(2)}, u32[]{:S(2)}) collective-permute-start(bf16[256,1536]{1,0:T(8,128)(2,1)} %pad_maximum_fusion.5), channel_id=1, source_target_pairs={{0,12},{1,13},{2,14},{3,15},{4,0},{5,1},{6,2},{7,3},{8,4},{9,5},{1... | collective-permute-start | bytes 2359304 | tf_op jit(solution)/shard_map/ppermute | solution.py:36
  (134 other events, 1500.8 us)
